TPU v7x, 512 devices: a whole 4x4x16 slice. The times are simulated.
512 devices in a mesh: seq: 128 (over y, z, core), head: 4 (over x).
Axes of the slice: x: 4, y: 4, z: 16, core: 2. Of those that a mesh axis runs over, the one named last changes fastest.
Arguments:
- stream: bfloat16 [16384, 5120], P('seq'), may hold values from -24 to 24
- queries: bfloat16 [16384, 2560], P('seq', 'head'), as said below
- keys: bfloat16 [16384, 2560], P('seq', 'head'), as said below
- values: bfloat16 [16384, 2560], P('seq', 'head'), may hold values from -6 to 6
- router_weight: bfloat16 [5120], replicated, may hold values from -0.111328125 to 0.111328125
- chosen: int32 [2048], replicated, may hold values from 0 to 16383, as said below
- owner: int32 [2048], replicated, may hold values from 0 to 127, as said below
- grad_out: bfloat16 [2048, 2560], P('seq', 'head'), may hold values from -6 to 6
Outputs:
- block_out: bfloat16 [2048, 2560], P('seq', 'head')
- grad_queries: bfloat16 [2048, 2560], P('seq', 'head')
- grad_keys: bfloat16 [2048, 2560], P('seq', 'head')
- grad_values: bfloat16 [2048, 2560], P('seq', 'head')
- grad_router: float32 [5120], P('seq')
Inputs may be any that keep to these rules, and one draw needn't show every extreme that they name: `chosen`: entries j * 16 to (j + 1) * 16 - 1 are distinct positions of tokens j * 128 to (j + 1) * 128 - 1, increasing. Every owner is named by exactly 16 rows. `queries`: entries lie between -240 and 240. `keys`: entries lie between -9 and 9.
All inputs are finite; a program needn't handle non-finite values.
Results may differ from a plain program's by a relative error of at most 0.017.
Values may be sent and summed in bfloat16 or wider, within the bound.
A program may use at most 64 MiB of HBM per device.

v0:
```python
import jax
import jax.numpy as jnp
from jax import lax
from jax.sharding import PartitionSpec as P

HEAD_DIM = 128


def split_heads(matrix):
    return matrix.reshape(matrix.shape[0], -1, HEAD_DIM)


def back_terms(
    slot_q, slot_pos, slot_grads, slot_total, slot_delta, own_k, own_v, owned_pos, head_scale
):
    back_scores = (
        jnp.einsum("shd,qhd->hsq", slot_q, own_k, preferred_element_type=jnp.float32) * head_scale
    )
    back_causal = slot_pos[:, None] >= owned_pos[None, :]
    back_scores = jnp.where(back_causal[None], back_scores, -jnp.inf)
    back_weights = jnp.exp(back_scores - slot_total.T[:, :, None]).astype(jnp.bfloat16)
    back_prob_grad = jnp.einsum(
        "shd,qhd->hsq", slot_grads, own_v, preferred_element_type=jnp.float32
    )
    back_score_grad = (
        back_weights.astype(jnp.float32) * (back_prob_grad - slot_delta.T[:, :, None])
    ).astype(jnp.bfloat16)
    grad_k = (
        jnp.einsum("hsq,shd->qhd", back_score_grad, slot_q, preferred_element_type=jnp.float32)
        * head_scale
    )
    grad_v = jnp.einsum(
        "hsq,shd->qhd", back_weights, slot_grads, preferred_element_type=jnp.float32
    )
    return (grad_k, grad_v)


def body(stream, queries, keys, values, router_weight, chosen, owner, grad_out):
    seq_index = lax.axis_index("seq")
    capacity = grad_out.shape[0]
    tok_rows = stream.shape[0]
    head_scale = HEAD_DIM ** (-0.5)
    local_rows = (
        lax.dynamic_slice_in_dim(chosen, seq_index * capacity, capacity) - seq_index * tok_rows
    )
    picked_q = jnp.take(queries, local_rows, axis=0)
    picked_k = jnp.take(keys, local_rows, axis=0)
    picked_v = jnp.take(values, local_rows, axis=0)
    picked_x = jnp.take(stream, local_rows, axis=0)
    router_logit = jnp.dot(picked_x, router_weight, preferred_element_type=jnp.float32).astype(
        jnp.bfloat16
    )
    all_q, all_k, all_v, all_logit = (
        lax.all_gather(picked_q, "seq", axis=0, tiled=True),
        lax.all_gather(picked_k, "seq", axis=0, tiled=True),
        lax.all_gather(picked_v, "seq", axis=0, tiled=True),
        lax.all_gather(router_logit, "seq", axis=0, tiled=True),
    )
    slot_rows = jnp.argsort(owner, stable=True)
    owned_rows = lax.dynamic_slice_in_dim(slot_rows, seq_index * capacity, capacity)
    owned_pos = jnp.take(chosen, owned_rows, axis=0)
    gating = jax.nn.sigmoid(jnp.take(all_logit, owned_rows, axis=0).astype(jnp.float32))
    own_q = split_heads(jnp.take(all_q, owned_rows, axis=0))
    own_k = split_heads(jnp.take(all_k, owned_rows, axis=0))
    own_v = split_heads(jnp.take(all_v, owned_rows, axis=0))
    key_k = split_heads(all_k)
    key_v = split_heads(all_v)
    scores = (
        jnp.einsum("qhd,khd->hqk", own_q, key_k, preferred_element_type=jnp.float32) * head_scale
    )
    causal = owned_pos[:, None] >= chosen[None, :]
    scores = jnp.where(causal[None], scores, -jnp.inf)
    row_max = jnp.max(scores, axis=2, keepdims=True)
    log_total = row_max + jnp.log(jnp.sum(jnp.exp(scores - row_max), axis=2, keepdims=True))
    weights = jnp.exp(scores - log_total).astype(jnp.bfloat16)
    context = jnp.einsum("hqk,khd->qhd", weights, key_v, preferred_element_type=jnp.float32)
    flat_ctx = context.reshape(capacity, -1)
    block_out = (gating[:, None] * flat_ctx).astype(jnp.bfloat16)
    upstream = grad_out.astype(jnp.float32)
    gate_part = jnp.sum(upstream * flat_ctx, axis=1)
    gate_slope = gating * (1.0 - gating)
    ctx_grad = (gating[:, None] * upstream).astype(jnp.bfloat16)
    grad_heads = split_heads(ctx_grad)
    row_delta = jnp.sum(grad_heads.astype(jnp.float32) * context, axis=2)
    logit_grad = lax.psum(gate_part, "head") * gate_slope
    prob_grad = jnp.einsum("qhd,khd->hqk", grad_heads, key_v, preferred_element_type=jnp.float32)
    score_grad = (weights.astype(jnp.float32) * (prob_grad - row_delta.T[:, :, None])).astype(
        jnp.bfloat16
    )
    grad_q = (
        jnp.einsum("hqk,khd->qhd", score_grad, key_k, preferred_element_type=jnp.float32)
        * head_scale
    )
    grad_queries = grad_q.reshape(capacity, -1).astype(jnp.bfloat16)
    row_totals = log_total[:, :, 0].T
    all_grads = lax.all_gather(ctx_grad, "seq", axis=0, tiled=True)
    all_total, all_delta, all_logit_grad = (
        lax.all_gather(row_totals, "seq", axis=0, tiled=True),
        lax.all_gather(row_delta, "seq", axis=0, tiled=True),
        lax.all_gather(logit_grad, "seq", axis=0, tiled=True),
    )
    slot_q = split_heads(jnp.take(all_q, slot_rows, axis=0))
    slot_pos = jnp.take(chosen, slot_rows, axis=0)
    grad_k, grad_v = back_terms(
        slot_q,
        slot_pos,
        split_heads(all_grads),
        all_total,
        all_delta,
        own_k,
        own_v,
        owned_pos,
        head_scale,
    )
    grad_keys = grad_k.reshape(capacity, -1).astype(jnp.bfloat16)
    grad_values = grad_v.reshape(capacity, -1).astype(jnp.bfloat16)
    slot_of_row = jnp.argsort(slot_rows)
    source_slots = lax.dynamic_slice_in_dim(slot_of_row, seq_index * capacity, capacity)
    source_grad = jnp.take(all_logit_grad, source_slots, axis=0)
    router_part = jnp.dot(
        source_grad[None, :], picked_x.astype(jnp.float32), precision=lax.Precision.HIGHEST
    )[0]
    grad_router = lax.psum_scatter(router_part, "seq", scatter_dimension=0, tiled=True)
    return (block_out, grad_queries, grad_keys, grad_values, grad_router)


def solution(mesh):
    return jax.shard_map(
        body,
        mesh=mesh,
        in_specs=(
            P("seq", None),
            P("seq", "head"),
            P("seq", "head"),
            P("seq", "head"),
            P(),
            P(),
            P(),
            P("seq", "head"),
        ),
        out_specs=(
            P("seq", "head"),
            P("seq", "head"),
            P("seq", "head"),
            P("seq", "head"),
            P("seq"),
        ),
        check_vma=False,
    )
```

profile of v0, /device:TPU:1, one launch (start us, length us, event | category | flops | bytes accessed | tf_op | source)
XLA Modules:
  0.0 1431.9 jit_solution(13246581949041929755)
XLA Ops:
  7.3 0.9 compare_and_fusion.1
  8.1 1.5 gather_fusion.7
  9.7 1.5 gather_fusion.9
  11.2 1.5 gather_fusion.6
  12.7 0.7 broadcast_select_fusion.13
  13.5 0.7 all-gather.9.cloned.1.call-update
  14.3 0.7 all-gather.11.cloned.1.call-update
  15.0 5.7 sort.34
  20.8 1.4 gather_fusion.2
  22.2 0.7 reshape.314
  22.9 0.6 gather_fusion
  23.6 0.6 fusion.57
  24.9 0.2 fusion.20
  25.1 0.2 dynamic-update-slice
  25.3 255.2 %all-reduce = bf16[2048]{0:T(1024)(128)(2,1)S(1)} all-reduce(bf16[2048]{0:T(1024)(128)(2,1)S(1)} %dynamic-update-slice), channel_id=1, replica_groups=mesh['seq'=128,'head'=4] {'seq'}, use_global_device_ids=true, to_apply=%add | all-reduce | flops 2048 | bytes 8192
  280.5 0.7 gather_fusion.1
  281.3 2.7 gather_fusion.11
  284.0 16.2 %all-gather.9.cloned.1.call-done = bf16[2048,640]{1,0:T(8,128)(2,1)} async-done(((bf16[16,640]{1,0:T(8,128)(2,1)}), bf16[2048,640]{1,0:T(8,128)(2,1)}) %all-gather.9.cloned.1.call-update) | async-done | bytes 2621456 | tf_op jit(solution)/shard_map/all_gather | solution.py:54
  300.2 2.7 gather_fusion.8
  302.9 137.5 %all-gather.11.cloned.1.call-done = bf16[2048,640]{1,0:T(8,128)(2,1)} async-done(((bf16[16,640]{1,0:T(8,128)(2,1)}), bf16[2048,640]{1,0:T(8,128)(2,1)}) %all-gather.11.cloned.1.call-update) | async-done | bytes 2621456 | tf_op jit(solution)/shard_map/all_gather | solution.py:55
  440.4 2.7 gather_fusion.10
  443.2 4.5 copy.36
  447.7 2.3 fusion.58
  449.9 0.2 exponential_reduce_fusion
  450.2 4.6 copy.35
  454.8 2.6 fusion.25
  457.5 8.4 psum.7
  466.0 0.7 fusion.27
  466.8 11.8 gather_fusion.4
  478.6 5.0 sort.35
  484.5 3.7 fusion.19
  488.2 0.6 copy.100
  488.9 11.6 gather_fusion.3
  500.5 4.5 copy.46
  505.0 83.7 %all-gather = f32[128,16,5]{1,2,0:T(8,128)S(1)} all-gather(f32[1,16,5]{1,2,0:T(8,128)S(1)} %bitcast.103), channel_id=1, replica_groups=mesh['seq'=128,'head'=4] {'seq'}, dimensions={0}, use_global_device_ids=true | all-gather | bytes 41280 | tf_op jit(solution)/shard_map/all_gather | solution.py:98
  588.8 0.2 reshape.295
  589.0 81.9 %all-gather.1 = f32[128,16,5]{1,2,0:T(8,128)S(1)} all-gather(f32[1,16,5]{1,2,0:T(8,128)S(1)} %bitcast.105), channel_id=1, replica_groups=mesh['seq'=128,'head'=4] {'seq'}, dimensions={0}, use_global_device_ids=true | all-gather | bytes 41280 | tf_op jit(solution)/shard_map/all_gather | solution.py:99
  671.0 0.2 reshape.297
  671.1 250.4 %all-reduce.1 = f32[2048]{0:T(1024)S(1)} all-reduce(f32[2048]{0:T(1024)S(1)} %get-tuple-element.11), channel_id=1, replica_groups=mesh['seq'=128,'head'=4] {'seq'}, use_global_device_ids=true, to_apply=%add.1 | all-reduce | flops 2048 | bytes 16384
  921.5 0.7 gather_fusion.5
  922.2 0.3 fusion.26
  922.5 488.5 %all-reduce.2 = f32[5120]{0:T(1024)S(1)} all-reduce(f32[5120]{0:T(1024)S(1)} %bitcast.107), channel_id=2, replica_groups=mesh['seq'=128,'head'=4] {'seq'}, use_global_device_ids=true, to_apply=%region_7.10.clone | all-reduce | flops 5120 | bytes 40960
  1411.0 0.6 dynamic-slice.3
  1411.6 2.4 fusion.8
  1414.0 4.5 copy.50
  1418.5 2.5 fusion.17
  1421.1 3.7 fusion.18
  1424.7 0.6 copy_bitcast_fusion
  (39 shorter events, 1.2 us)
Async XLA Ops:
  7.2 15.8 %copy-start = (bf16[128,5120]{1,0:T(8,128)(2,1)S(1)}, bf16[128,5120]{1,0:T(8,128)(2,1)}, u32[]{:S(2)}) copy-start(bf16[128,5120]{1,0:T(8,128)(2,1)} %param.12) | copy-start | bytes 3932164
  7.2 16.4 %copy-start.4 = (u32[512]{0:T(512)S(1)}, u32[512]{0:T(512)}, u32[]{:S(2)}) copy-start(u32[512]{0:T(512)} %constant.124) | copy-start | bytes 6148
  7.2 274.0 %copy-start.1 = (s32[2048]{0:T(1024)S(1)}, s32[2048]{0:T(1024)}, u32[]{:S(2)}) copy-start(s32[2048]{0:T(1024)} %param.17) | copy-start | bytes 24580
  7.2 274.1 %all-gather.7.cloned.1.call-start = ((), (), s32[]{:S(2)}) async-start(), calls=%async_computation | async-start | bytes 2641920 | tf_op jit(solution)/shard_map/all_gather | solution.py:56
  13.5 286.7 %all-gather.9.cloned.1.call-start = ((), (), s32[]{:S(2)}) async-start(), calls=%async_computation.1 | async-start | bytes 2641920 | tf_op jit(solution)/shard_map/all_gather | solution.py:54
  14.2 426.2 %all-gather.11.cloned.1.call-start = ((), (), s32[]{:S(2)}) async-start(), calls=%async_computation.2 | async-start | bytes 2641920 | tf_op jit(solution)/shard_map/all_gather | solution.py:55
  15.0 1399.1 %all-gather.13.cloned.1.call-start = ((), (), s32[]{:S(2)}) async-start(), calls=%async_computation.3 | async-start | bytes 2641920 | tf_op jit(solution)/shard_map/all_gather | solution.py:96
  454.8 2.6 copy-start.3
  466.8 17.7 %copy-start.2 = (bf16[16,640]{1,0:T(8,128)(2,1)S(1)}, bf16[16,640]{1,0:T(8,128)(2,1)}, u32[]{:S(2)}) copy-start(bf16[16,640]{1,0:T(8,128)(2,1)} %get-tuple-element.24) | copy-start | bytes 61444
Sparse Core Ops, SparseCore 0:
  13.6 146.3 all-gather.6
  163.6 136.5 all-gather.8
  303.8 136.5 all-gather.10
  466.9 136.7 all-gather.12
where the time goes:
time: 1440 us; the launch traced here: 1430 us
  blocking collectives  1170 us (81%)
  waiting for transfers between devices  155 us (11%)
  local copies, waits for them, and re-layouts  61.4 us (4%)
  matrix products  17.7 us (1%)
  between operations  15.3 us (1%)
    unnamed x3, blocking collectives  994 us
    all_gather x1, waiting for transfers between devices, body(): lax.all_gather(picked_k, 'seq', axis=0, tiled=True)  138 us
    all_gather x1, blocking collectives, body(): lax.all_gather(row_totals, 'seq', axis=0, tiled=True)  83.7 us
    all_gather x1, blocking collectives, body(): lax.all_gather(row_delta, 'seq', axis=0, tiled=True)  81.9 us
  transfers between devices with their start and end apart: 4, of which 2 were waited for; matrix products, arithmetic and copies ran while one was open for 4% of the time, Pallas kernels for 0%

commit v1 on v0

v1 whole, which is shorter than its diff:
```python
import jax
import jax.numpy as jnp
from jax import lax
from jax.experimental import pallas as pl
from jax.experimental.pallas import tpu as pltpu
from jax.sharding import PartitionSpec as P

NY, NZ, NX = 4, 16, 4
CAP = 16
HD = 128
ROWS = 2048
SCALE = HD**-0.5
MESH = pl.DeviceIdType.MESH
Q, K, G, V = 0, 1, 2, 3
F32, BF16 = jnp.float32, jnp.bfloat16


def dot(a, b, ca, cb):
    return lax.dot_general(a, b, (((ca,), (cb,)), ((), ())), preferred_element_type=F32)


def iota(shape, dim):
    return lax.broadcasted_iota(jnp.int32, shape, dim)


def kernel(
    chosen_ref, owner_ref, weight_ref, q_ref, k_ref, v_ref, g_ref, stream_ref,
    block_out_ref, gq_ref, gk_ref, gv_ref, router_ref,
    xs, pk, gat, xc, xt, ltile, lplane, lall, lsum,
    slot, pt, sel, ownx, st, wt, vt, gct, gc, rows, ob, outs,
    xg, gps, lgp, part, pr, fx,
    sem_x, p1s, p1r, ls, lr, rs, rr, fs, fr, dls, dlr, xts, xtr, outsem_s, outsem_r,
    xgs, xgr, gs, gr, prs, prr, fxs, fxr,
):
    seq, x = lax.axis_index("seq"), lax.axis_index("head")
    y, z, c = seq // 32, (seq // 2) % NZ, seq % 2
    me = y * 2 + c
    is_owner = (c == 0) | (y == 0)
    head = y * (1 - c) + 4 * c

    def dev(yy, zz, cc, xx):
        return (yy * 32 + zz * 2 + cc, xx)

    def remote(src, dst, ss, rsem, target):
        return pltpu.make_async_remote_copy(
            src_ref=src, dst_ref=dst, send_sem=ss, recv_sem=rsem, device_id=target, device_id_type=MESH
        )

    stream_copy = pltpu.make_async_copy(stream_ref, xs, sem_x)
    stream_copy.start()
    xt[...] = jnp.zeros_like(xt)

    plane = []
    for i in range(1, 8):
        p = (me + i) % 8
        plane.append((p // 2, p % 2))
    peers = [dev(yy, z, cc, x) for yy, cc in plane]
    peers += [dev(y, (z + i) % NZ, c, x) for i in range(1, NZ)]
    peers += [dev(y, z, c, (x + i) % NX) for i in range(1, NX)]
    barrier = pltpu.get_barrier_semaphore()
    for p in peers:
        pl.semaphore_signal(barrier, inc=1, device_id=p, device_id_type=MESH)

    token = jnp.zeros((CAP, 128), jnp.int32)
    for r in range(CAP):
        token = jnp.where(iota((CAP, 128), 0) == r, chosen_ref[seq * CAP + r] - seq * 128, token)
    pick = (token == iota((CAP, 128), 1)).astype(BF16)
    pk[Q] = dot(pick, q_ref[...], 1, 0).astype(BF16)
    pk[K] = dot(pick, k_ref[...], 1, 0).astype(BF16)
    pk[V] = dot(pick, v_ref[...], 1, 0).astype(BF16)
    pk[G] = g_ref[...]

    pl.semaphore_wait(barrier, len(peers))

    my_rows = pl.ds(pl.multiple_of(c * CAP, CAP), CAP)

    def to_head(h, target):
        return remote(
            pk.at[:, :, pl.ds(h * HD, HD)], gat.at[:, y, z, my_rows, :], p1s.at[h], p1r.at[me], target
        )

    for h in range(4):
        here = (c == 0) & (y == h)

        @pl.when(jnp.logical_not(here))
        def _():
            to_head(h, dev(h, z, 0, x)).start()

        @pl.when(here)
        def _():
            gat[:, y, z, my_rows, :] = pk[:, :, h * HD : (h + 1) * HD]

    @pl.when(c == 0)
    def _():
        to_head(4, dev(y, z, 1, x)).start()

    @pl.when(c == 1)
    def _():
        gat[:, y, z, my_rows, :] = pk[:, :, 4 * HD : 5 * HD]

    stream_copy.wait()
    for t in range(5):
        cols = slice(t * 1024, (t + 1) * 1024)
        xc[:, cols] = dot(pick, xs[:, cols], 1, 0).astype(BF16)
    xc[:, 5120:] = jnp.zeros((CAP, 128), BF16)
    logit = jnp.sum(xc[:, :5120].astype(F32) * weight_ref[...].astype(F32), axis=1, keepdims=True)
    spread = jnp.where(
        iota((CAP, 128), 1) == (seq % 8) * CAP + iota((CAP, 128), 0), logit, jnp.zeros((), F32)
    )
    line = jnp.sum(spread, axis=0, keepdims=True)
    ltile[...] = jnp.where(iota((16, 128), 0) == seq // 8, line, jnp.zeros((), F32)).astype(BF16)

    def to_logit(h):
        return remote(ltile, lplane.at[me], ls.at[h], lr.at[me], dev(h, z, 0, x))

    for h in range(4):
        here = (c == 0) & (y == h)

        @pl.when(jnp.logical_not(here))
        def _():
            to_logit(h).start()

        @pl.when(here)
        def _():
            lplane[me] = ltile[...]

    def window(zz):
        return pl.ds(pl.multiple_of(x * 1280 + (zz * 80 // 128) * 128, 128), 256)

    xt_rows = pl.ds(pl.multiple_of(z * 32 + c * CAP, CAP), CAP)

    def ring_core0(a, s, d, ahead=0):
        zz = (z - s - ahead + 2 * NZ) % NZ if d == 0 else (z + s + ahead) % NZ
        ref = lall.at[zz] if a == 4 else gat.at[a, :, zz]
        to = (z + 1) % NZ if d == 0 else (z + NZ - 1) % NZ
        return remote(ref, ref, rs.at[d, a, s], rr.at[d, a, s], dev(y, to, c, x))

    def ring_core1(a, s, d, ahead=0):
        zz = (z - s - ahead + 2 * NZ) % NZ if d == 0 else (z + s + ahead) % NZ
        ref = gat.at[a, y, zz]
        to = (z + 1) % NZ if d == 0 else (z + NZ - 1) % NZ
        return remote(ref, ref, rs.at[d, a, s], rr.at[d, a, s], dev(y, to, c, x))

    def forward(zz, k):
        ref = gat.at[:, y, zz]
        return remote(ref, ref, fs.at[k], fr.at[y - 1, zz], dev(0, z, 1, x))

    steps = (8, 7)

    @pl.when(c == 0)
    def _():
        for p in range(8):
            yy, cc = p // 2, p % 2

            @pl.when(p != me)
            def _():
                got = gat.at[:, yy, z, pl.ds(cc * CAP, CAP), :]
                remote(got, got, p1s.at[0], p1r.at[p], dev(yy, z, cc, x)).wait_recv()

        for a in range(4):
            for d in (0, 1):
                ring_core0(a, 0, d).start()
        total = jnp.zeros((16, 128), F32)
        for p in range(8):

            @pl.when(p != me)
            def _():
                remote(ltile, lplane.at[p], ls.at[0], lr.at[p], dev(p // 2, z, p % 2, x)).wait_recv()

        for p in range(8):
            total = total + lplane[p].astype(F32)
        lall[z] = total.astype(BF16)
        for d in (0, 1):
            ring_core0(4, 0, d).start()
        for s in range(1, 9):
            for a in range(5):
                for d in (0, 1):
                    if s - 1 < steps[d]:
                        ring_core0(a, s - 1, d, 1).wait_recv()
                    if s < steps[d]:
                        ring_core0(a, s, d).start()

    @pl.when(c == 1)
    def _():
        got = gat.at[:, y, z, pl.ds(0, CAP), :]
        remote(got, got, p1s.at[0], p1r.at[y * 2], dev(y, z, 0, x)).wait_recv()
        for a in range(4):
            for d in (0, 1):
                ring_core1(a, 0, d).start()

        @pl.when(y != 0)
        def _():
            forward(z, 0).start()

        for s in range(1, 9):
            for a in range(4):
                for d in (0, 1):
                    if s - 1 < steps[d]:
                        ring_core1(a, s - 1, d, 1).wait_recv()
                    if s < steps[d]:
                        ring_core1(a, s, d).start()

            @pl.when(y != 0)
            def _():
                forward((z - s + 2 * NZ) % NZ, s).start()
                if s - 1 < steps[1]:
                    forward((z + s) % NZ, 8 + s).start()

        @pl.when(y == 0)
        def _():
            for yy in range(1, 4):
                for zz in range(NZ):
                    ref = gat.at[:, yy, zz]
                    remote(ref, ref, fs.at[0], fr.at[yy - 1, zz], dev(yy, z, 1, x)).wait_recv()

    def to_column(i):
        zz = (z + i) % NZ
        return remote(xc.at[:, window(zz)], xt.at[xt_rows, :], xts.at[i], xtr.at[z], dev(y, zz, c, x))

    for i in range(1, NZ):
        to_column(i).start()
    xt[xt_rows, :] = xc[:, window(z)]

    @pl.when(c == 0)
    def _():
        total = jnp.zeros((16, 128), F32)
        for zz in range(NZ):
            total = total + lall[zz].astype(F32)
        lsum[...] = total

    def to_sibling():
        return remote(lsum, lsum, dls, dlr, dev(0, z, 1, x))

    @pl.when((c == 0) & (y == 0))
    def _():
        to_sibling().start()

    @pl.when((c == 1) & (y == 0))
    def _():
        to_sibling().wait_recv()

    def all_rows(a):
        return gat[a].reshape(ROWS, HD)

    def to_slot_owner(i):
        yy, cc = plane[i - 1]
        mine = pl.ds(pl.multiple_of(yy * 32 + cc * CAP, CAP), CAP)
        return remote(
            ob.at[:, mine, :],
            outs.at[:, :, pl.ds(pl.multiple_of(head * HD, HD), HD)],
            outsem_s.at[i], outsem_r.at[head], dev(yy, z, cc, x),
        )

    def to_x(i):
        return remote(xg.at[x], xg.at[x], xgs.at[i], xgr.at[x], dev(y, z, c, (x + i) % NX))

    def to_plane(i):
        yy, cc = plane[i - 1]
        return remote(gps.at[yy], lgp.at[head], gs.at[i], gr.at[head], dev(yy, z, cc, x))

    @pl.when(is_owner)
    def _():
        sub = iota((128, 128), 0)
        lane = iota((128, 128), 1)
        before = (sub < lane).astype(BF16)
        base = jnp.zeros((128, 1), F32)
        for t in range(16):
            line = owner_ref[t : t + 1, :]
            names = (sub == line).astype(F32)
            count = dot(names.astype(BF16), before, 1, 0)
            rank = jnp.sum(names * (count + base), axis=0, keepdims=True)
            base = base + jnp.sum(names, axis=1, keepdims=True)
            slot[t : t + 1, :] = line.astype(F32) * 16.0 + rank
        slot[16:, :] = jnp.zeros((112, 128), F32)
        slot_col = jnp.transpose(slot[...])
        own_slot = ((sub // 32) * 512 + z * 32 + sub % 32).astype(F32)
        for t in range(16):
            cols = slice(t * 128, (t + 1) * 128)
            sel[:, cols] = (own_slot == slot[t : t + 1, :]).astype(BF16)
            column = jnp.broadcast_to(slot_col[:, t : t + 1], (128, 128))
            for u in range(16):
                pt[cols, u * 128 : (u + 1) * 128] = (column == (lane + u * 128).astype(F32)).astype(BF16)
            row16 = iota((16, 128), 0)
            lane16 = iota((16, 128), 1)
            value = jnp.where(row16 == 0, t * 8 + lane16 // 16, jnp.where(row16 == 1, lane16 % 16, 0))
            ownx[:, cols] = jnp.where(row16 == 2, lsum[t : t + 1, :], value.astype(F32)).astype(BF16)
            gating = jax.nn.sigmoid(lsum[t : t + 1, :])
            rows[2:3, cols] = gating
        own = dot(sel[...], ownx[...], 1, 1)
        own_j = own[:, 0:1] * 16.0 + own[:, 1:2]
        own_j_row = jnp.transpose(jnp.broadcast_to(own_j, (128, 128)))[0:1]
        own_logit_row = jnp.transpose(jnp.broadcast_to(own[:, 2:3], (128, 128)))[0:1]
        own_gate = jax.nn.sigmoid(own_logit_row)

        selw = sel[...]
        q_own = dot(selw, all_rows(Q), 1, 0).astype(BF16)
        k_own = dot(selw, all_rows(K), 1, 0).astype(BF16)
        v_own = dot(selw, all_rows(V), 1, 0).astype(BF16)
        g_own = gat[G, :, z].reshape(128, HD)

        vt[...] = jnp.transpose(all_rows(V))
        for t in range(4):
            part_rows = slice(t * 512, (t + 1) * 512)
            block = dot(pt[part_rows, :], all_rows(G), 1, 0)
            gc[part_rows, :] = block.astype(BF16)
            gct[:, part_rows] = jnp.transpose(block)

        for t in range(4):
            cols = slice(t * 512, (t + 1) * 512)
            q_block = gat[Q, t].reshape(512, HD)
            most = jnp.full((1, 512), -jnp.inf, F32)
            for u in range(t + 1):
                score = dot(gat[K, u].reshape(512, HD), q_block, 1, 1)
                if u == t:
                    score = jnp.where(iota((512, 512), 0) <= iota((512, 512), 1), score, -jnp.inf)
                st[u * 512 : (u + 1) * 512, :] = score
                most = jnp.maximum(most, jnp.max(score, axis=0, keepdims=True))
            total = jnp.zeros((1, 512), F32)
            for u in range(t + 1):
                keys = slice(u * 512, (u + 1) * 512)
                weight = jnp.exp((st[keys, :] - most) * SCALE)
                total = total + jnp.sum(weight, axis=0, keepdims=True)
                wt[keys, :] = weight.astype(BF16)
            n = (t + 1) * 512
            ctx = dot(vt[:, :n], wt[:n, :], 1, 0)
            gate_part = jnp.sum(ctx * gct[:, cols], axis=0, keepdims=True) / total
            gating = rows[2:3, cols]
            rows[0:1, cols] = most * SCALE + jnp.log(total)
            rows[1:2, cols] = gating * gate_part
            logit_grad = gate_part * gating * (1.0 - gating)
            for u in range(4):
                xg[x, t, u : u + 1, :] = logit_grad[:, u * 128 : (u + 1) * 128]
            xg[x, t, 4:8, :] = jnp.zeros((4, 128), F32)
        for i in range(1, NX):
            to_x(i).start()

        score = dot(all_rows(K), q_own, 1, 1)
        score = jnp.where(iota((ROWS, 128), 0).astype(F32) <= own_j_row, score, -jnp.inf)
        most = jnp.max(score, axis=0, keepdims=True)
        weight = jnp.exp((score - most) * SCALE)
        weight = (weight * (1.0 / jnp.sum(weight, axis=0, keepdims=True))).astype(BF16)
        ctx = dot(vt[...], weight, 1, 0)
        g_own_t = jnp.transpose(g_own.astype(F32))
        delta = jnp.sum(ctx * g_own_t, axis=0, keepdims=True) * own_gate
        ob[0] = jnp.transpose(ctx * own_gate).astype(BF16)
        prob_grad = dot(all_rows(V), g_own, 1, 1) * own_gate
        score_grad = (weight.astype(F32) * (prob_grad - delta)).astype(BF16)
        ob[1] = (dot(score_grad, all_rows(K), 0, 0) * SCALE).astype(BF16)

        score = dot(k_own, all_rows(Q), 1, 1) * SCALE
        causal = iota((128, ROWS), 1).astype(F32) >= own_j
        weight = jnp.exp(jnp.where(causal, score - rows[0:1, :], -jnp.inf)).astype(BF16).astype(F32)
        prob_grad = dot(v_own, gc[...], 1, 1) * rows[2:3, :]
        score_grad = (weight * (prob_grad - rows[1:2, :])).astype(BF16)
        ob[2] = (dot(score_grad, all_rows(Q), 1, 0) * SCALE).astype(BF16)
        ob[3] = dot((weight * rows[2:3, :]).astype(BF16), gc[...], 1, 0).astype(BF16)
        for i in range(1, 8):
            to_slot_owner(i).start()
        here = pl.ds(pl.multiple_of(y * 32 + c * CAP, CAP), CAP)
        outs[:, :, pl.ds(pl.multiple_of(head * HD, HD), HD)] = ob[:, here, :]

        for i in range(1, NX):
            xx = (x + i) % NX
            remote(xg.at[xx], xg.at[xx], xgs.at[0], xgr.at[xx], dev(y, z, c, xx)).wait_recv()
        gps[...] = xg[0] + xg[1] + xg[2] + xg[3]
        for i in range(1, 8):
            to_plane(i).start()
        lgp[head] = gps[y]

    for h in range(5):
        yy, cc = (h, 0) if h < 4 else (0, 1)

        @pl.when((yy != y) | (cc != c))
        def _():
            remote(lgp.at[h], lgp.at[h], gs.at[0], gr.at[h], dev(yy, z, cc, x)).wait_recv()

    for i in range(1, NZ):
        zz = (z + i) % NZ
        got = xt.at[pl.ds(pl.multiple_of(zz * 32 + c * CAP, CAP), CAP), :]
        remote(got, got, xts.at[0], xtr.at[zz], dev(y, zz, c, x)).wait_recv()
    logit_grad = lgp[0] + lgp[1] + lgp[2] + lgp[3] + lgp[4]
    total = jnp.zeros((8, 256), F32)
    for t in range(4):
        line = jnp.broadcast_to(logit_grad[t : t + 1, :], (8, 128))
        total = total + lax.dot_general(
            line, xt[t * 128 : (t + 1) * 128, :].astype(F32), (((1,), (0,)), ((), ())),
            precision=lax.Precision.HIGHEST, preferred_element_type=F32,
        )
    part[...] = total

    def to_part(cc):
        return remote(part, pr.at[me], prs.at[cc], prr.at[me], dev(x, z, cc, x))

    def to_fx(i):
        return remote(part, fx, fxs.at[i], fxr, dev(y, z, c, (x + i) % NX))

    for cc in range(2):

        @pl.when((y != x) | (c != cc))
        def _():
            to_part(cc).start()

    @pl.when(y == x)
    def _():
        pr[me] = part[...]
        for p in range(8):

            @pl.when(p != me)
            def _():
                remote(pr.at[p], pr.at[p], prs.at[0], prr.at[p], dev(p // 2, z, p % 2, x)).wait_recv()

        to_part(1 - c).wait_send()
        total = pr[0]
        for p in range(1, 8):
            total = total + pr[p]
        part[...] = total
        fx[...] = total
        for i in range(1, NX):
            to_fx(i).start()

    @pl.when(y != x)
    def _():
        remote(part, fx, fxs.at[0], fxr, dev(y, z, c, y)).wait_recv()

    offset = (z * 80) % 128 + c * 40
    router_ref[...] = pltpu.roll(fx[...], (256 - offset) % 256, 1)[:, :128]

    for h in range(5):
        yy, cc = (h, 0) if h < 4 else (0, 1)

        @pl.when((yy != y) | (cc != c))
        def _():
            got = outs.at[:, :, pl.ds(h * HD, HD)]
            remote(got, got, outsem_s.at[0], outsem_r.at[h], dev(yy, z, cc, x)).wait_recv()

    block_out_ref[...] = outs[0]
    gq_ref[...] = outs[1]
    gk_ref[...] = outs[2]
    gv_ref[...] = outs[3]

    for h in range(4):

        @pl.when((c != 0) | (y != h))
        def _():
            to_head(h, dev(h, z, 0, x)).wait_send()
            to_logit(h).wait_send()

    @pl.when(c == 0)
    def _():
        to_head(4, dev(y, z, 1, x)).wait_send()
        for s in range(8):
            for a in range(5):
                for d in (0, 1):
                    if s < steps[d]:
                        ring_core0(a, s, d).wait_send()

    @pl.when(c == 1)
    def _():
        for s in range(8):
            for a in range(4):
                for d in (0, 1):
                    if s < steps[d]:
                        ring_core1(a, s, d).wait_send()

        @pl.when(y != 0)
        def _():
            for k in range(16):
                forward(z, k).wait_send()

    @pl.when((c == 0) & (y == 0))
    def _():
        to_sibling().wait_send()

    for i in range(1, NZ):
        to_column(i).wait_send()

    @pl.when(is_owner)
    def _():
        for i in range(1, 8):
            to_slot_owner(i).wait_send()
            to_plane(i).wait_send()
        for i in range(1, NX):
            to_x(i).wait_send()

    @pl.when(y != x)
    def _():
        to_part(0).wait_send()
        to_part(1).wait_send()

    @pl.when(y == x)
    def _():
        for i in range(1, NX):
            to_fx(i).wait_send()


def body(stream, queries, keys, values, router_weight, chosen, owner, grad_out):
    vmem = pl.BlockSpec(memory_space=pltpu.VMEM)
    dma = pltpu.SemaphoreType.DMA
    wide = jax.ShapeDtypeStruct((CAP, 5 * HD), BF16)
    scratch = [
        pltpu.VMEM((128, 5120), BF16),
        pltpu.VMEM((4, CAP, 5 * HD), BF16),
        pltpu.VMEM((4, NY, NZ, 32, HD), BF16),
        pltpu.VMEM((CAP, 5248), BF16),
        pltpu.VMEM((512, 256), BF16),
        pltpu.VMEM((16, 128), BF16),
        pltpu.VMEM((8, 16, 128), BF16),
        pltpu.VMEM((NZ, 16, 128), BF16),
        pltpu.VMEM((16, 128), F32),
        pltpu.VMEM((128, 128), F32),
        pltpu.VMEM((ROWS, ROWS), BF16),
        pltpu.VMEM((128, ROWS), BF16),
        pltpu.VMEM((16, ROWS), BF16),
        pltpu.VMEM((ROWS, 512), F32),
        pltpu.VMEM((ROWS, 512), BF16),
        pltpu.VMEM((HD, ROWS), BF16),
        pltpu.VMEM((HD, ROWS), F32),
        pltpu.VMEM((ROWS, HD), BF16),
        pltpu.VMEM((8, ROWS), F32),
        pltpu.VMEM((4, 128, HD), BF16),
        pltpu.VMEM((4, CAP, 5 * HD), BF16),
        pltpu.VMEM((NX, NY, 8, 128), F32),
        pltpu.VMEM((NY, 8, 128), F32),
        pltpu.VMEM((5, 8, 128), F32),
        pltpu.VMEM((8, 256), F32),
        pltpu.VMEM((8, 8, 256), F32),
        pltpu.VMEM((8, 256), F32),
        dma, dma((5,)), dma((8,)), dma((4,)), dma((8,)),
        dma((2, 5, 8)), dma((2, 5, 8)), dma((16,)), dma((3, 16)), dma, dma,
        dma((16,)), dma((16,)), dma((8,)), dma((5,)),
        dma((4,)), dma((4,)), dma((8,)), dma((5,)), dma((2,)), dma((8,)), dma((4,)), dma,
    ]
    *big, router = pl.pallas_call(
        kernel,
        out_shape=(wide, wide, wide, wide, jax.ShapeDtypeStruct((8, 128), F32)),
        in_specs=[pl.BlockSpec(memory_space=pltpu.SMEM)] + [vmem] * 6 + [pl.BlockSpec(memory_space=pl.ANY)],
        out_specs=(vmem,) * 5,
        scratch_shapes=scratch,
        compiler_params=pltpu.CompilerParams(
            collective_id=0, has_side_effects=True, vmem_limit_bytes=48 * 2**20
        ),
        name="routed_attention",
    )(
        chosen, owner.reshape(16, 128), router_weight.reshape(1, -1),
        queries, keys, values, grad_out, stream,
    )
    return (*big, router[0, :40])


def solution(mesh):
    return jax.shard_map(
        body,
        mesh=mesh,
        in_specs=(
            P("seq", None),
            P("seq", "head"),
            P("seq", "head"),
            P("seq", "head"),
            P(),
            P(),
            P(),
            P("seq", "head"),
        ),
        out_specs=(
            P("seq", "head"),
            P("seq", "head"),
            P("seq", "head"),
            P("seq", "head"),
            P("seq"),
        ),
        check_vma=False,
    )
```

time: 1440 us -> 86.3 us (0.06)
  blocking collectives: 1170 us -> 0 us
  waiting for transfers between devices: 155 us -> 0 us
  Pallas kernels: 0 us -> 74.8 us
  local copies, waits for them, and re-layouts: 61.4 us -> 9.83 us
  matrix products: 17.7 us -> 0 us
  between operations: 15.3 us -> 0.66 us
    unnamed x3 -> x0, blocking collectives: 994 us -> none
    all_gather x2 -> x0, blocking collectives: 166 us -> none  [the longest x1 83.7 us: body(): lax.all_gather(row_totals, 'seq', axis=0, tiled=True)]
    all_gather x4 -> x0, waiting for transfers between devices: 154 us -> none  [the longest x1 138 us: body(): lax.all_gather(picked_k, 'seq', axis=0, tiled=True)]
    pallas_call x0 -> x1, Pallas kernels: none -> 74.8 us  [body(): pl.pallas_call(kernel, out_shape=(wide, wide, wide, wide, jax.ShapeDtypeS...]
    gather x13 -> x0, local copies, waits for them, and re-layouts: 43.9 us -> none  [the longest x2 16.1 us: body(): slot_q = split_heads(jnp.take(all_q, slot_rows, axis=0))]
    dot_general x8 -> x0, matrix products: 17.7 us -> none  [the longest x1 3.68 us: body(): jnp.einsum('hqk,khd->qhd', score_grad, key_k, preferred_element_type=jnp....]
  transfers between devices with their start and end apart: 4 -> 0, of which waited for: 2 -> 0; matrix products, arithmetic and copies ran while one was open for 4% -> 0% of each run, Pallas kernels for 0% -> 0%
where the time goes in v1:
time: 86.3 us; the launch traced here: 85.3 us
  Pallas kernels  74.8 us (87%)
  local copies, waits for them, and re-layouts  9.83 us (11%)
    pallas_call x1, Pallas kernels, body(): pl.pallas_call(kernel, out_shape=(wide, wide, wide, wide, jax.ShapeDtypeS...  74.8 us
    unnamed x18, local copies, waits for them, and re-layouts  8.6 us

profile of v1, /device:TPU:1, one launch (start us, length us, event | category | flops | bytes accessed | tf_op | source)
XLA Modules:
  0.0 85.3 jit_solution(6604548409522287909)
XLA Ops:
  0.6 0.7 reshape.17.weight_ref
  1.3 0.0 copy-start
  1.4 1.3 %copy-done = bf16[128,5120]{1,0:T(8,128)(2,1)S(1)} copy-done((bf16[128,5120]{1,0:T(8,128)(2,1)S(1)}, bf16[128,5120]{1,0:T(8,128)(2,1)}, u32[]{:S(2)}) %copy-start) | copy-done | bytes 1310744
  2.7 0.0 copy-start.1
  2.7 0.9 %copy-done.1 = bf16[128,640]{1,0:T(8,128)(2,1)S(1)} copy-done((bf16[128,640]{1,0:T(8,128)(2,1)S(1)}, bf16[128,640]{1,0:T(8,128)(2,1)}, u32[]{:S(2)}) %copy-start.1) | copy-done | bytes 163864
  3.6 0.0 copy-start.2
  3.6 0.9 %copy-done.2 = bf16[128,640]{1,0:T(8,128)(2,1)S(1)} copy-done((bf16[128,640]{1,0:T(8,128)(2,1)S(1)}, bf16[128,640]{1,0:T(8,128)(2,1)}, u32[]{:S(2)}) %copy-start.2) | copy-done | bytes 163864
  4.5 0.0 copy-start.3
  4.5 0.9 %copy-done.3 = bf16[128,640]{1,0:T(8,128)(2,1)S(1)} copy-done((bf16[128,640]{1,0:T(8,128)(2,1)S(1)}, bf16[128,640]{1,0:T(8,128)(2,1)}, u32[]{:S(2)}) %copy-start.3) | copy-done | bytes 163864
  5.4 0.0 copy-start.4
  5.4 0.7 copy-done.4
  6.1 0.0 copy-start.5
  6.1 0.7 copy-done.5
  6.8 0.0 copy-start.6
  6.8 0.7 copy-done.6
  7.5 74.8 %routed_attention.1 = (bf16[16,640]{1,0:T(8,128)(2,1)S(1)}, bf16[16,640]{1,0:T(8,128)(2,1)S(1)}, bf16[16,640]{1,0:T(8,128)(2,1)S(1)}, bf16[16,640]{1,0:T(8,128)(2,1)S(1)}, f32[8,128]{1,0:T(8,128)S(1)}) custom-call(s32[2048]{0:T(1024)S(1)} %copy-done.5, s32[16,128]{1,0:T(8,128)S(1)} %bitcast.3, bf16[1,5120]{1,0:T(2,128)(2,1)S(1)} %reshape.17.weight_ref, ...), custom_call_target="tpu_custom_call" | custom-call | tf_op jit(solution)/shard_map/routed_attention/pallas_call | solution.py:533
  82.4 0.5 slice_bitcast_fusion
  82.9 0.6 copy.17
  83.5 0.6 copy.18
  84.1 0.6 copy.19
  84.7 0.6 copy.20
Async XLA Ops:
  1.3 1.3 %copy-start = (bf16[128,5120]{1,0:T(8,128)(2,1)S(1)}, bf16[128,5120]{1,0:T(8,128)(2,1)}, u32[]{:S(2)}) copy-start(bf16[128,5120]{1,0:T(8,128)(2,1)} %stream_ref.1) | copy-start | bytes 3932164
  2.7 0.9 %copy-start.1 = (bf16[128,640]{1,0:T(8,128)(2,1)S(1)}, bf16[128,640]{1,0:T(8,128)(2,1)}, u32[]{:S(2)}) copy-start(bf16[128,640]{1,0:T(8,128)(2,1)} %q_ref.1) | copy-start | bytes 491524
  3.6 0.9 %copy-start.2 = (bf16[128,640]{1,0:T(8,128)(2,1)S(1)}, bf16[128,640]{1,0:T(8,128)(2,1)}, u32[]{:S(2)}) copy-start(bf16[128,640]{1,0:T(8,128)(2,1)} %k_ref.1) | copy-start | bytes 491524
  4.5 0.9 %copy-start.3 = (bf16[128,640]{1,0:T(8,128)(2,1)S(1)}, bf16[128,640]{1,0:T(8,128)(2,1)}, u32[]{:S(2)}) copy-start(bf16[128,640]{1,0:T(8,128)(2,1)} %v_ref.1) | copy-start | bytes 491524
  5.4 0.7 copy-start.4
  6.1 0.7 copy-start.5
  6.8 0.7 copy-start.6

commit v2 on v1

v2 whole, which is shorter than its diff:
```python
import jax
import jax.numpy as jnp
from jax import lax
from jax.experimental import pallas as pl
from jax.experimental.pallas import tpu as pltpu
from jax.sharding import PartitionSpec as P

NY, NZ, NX = 4, 16, 4
CAP = 16
HD = 128
ROWS = 2048
SCALE = HD**-0.5
MESH = pl.DeviceIdType.MESH
Q, K, G, V = 0, 1, 2, 3
F32, BF16 = jnp.float32, jnp.bfloat16


def dot(a, b, ca, cb):
    return lax.dot_general(a, b, (((ca,), (cb,)), ((), ())), preferred_element_type=F32)


def iota(shape, dim):
    return lax.broadcasted_iota(jnp.int32, shape, dim)


def kernel(
    chosen_ref, owner_in, weight_in, q_in, k_in, v_in, g_in, stream_in,
    out_ref, router_ref,
    xs, qin, kin, vin, win, own_ref, pk, gat, ring, quarter, xc, xt, ltile, lplane, lall, lsum,
    slot, pt, sel, ownx, st, wt, wo, w2, vt, gct, gc, rows, ob, outs,
    gl, lgx, part, pr,
    sem_in, p1s, p1r, qr_s, qr_r, ls, lr, rs, rr, ffs, ffr, qfs, fr, dls, dlr, xts, xtr,
    outsem_s, outsem_r, gs, gr, prs, prr, xready,
):
    seq, x = lax.axis_index("seq"), lax.axis_index("head")
    y, z, c = seq // 32, (seq // 2) % NZ, seq % 2
    me = y * 2 + c
    is_owner = (c == 0) | (y == 0)
    head = y * (1 - c) + 4 * c
    mine = x * 5 + head

    def dev(yy, zz, cc, xx):
        return (yy * 32 + zz * 2 + cc, xx)

    def remote(src, dst, ss, rsem, target):
        return pltpu.make_async_remote_copy(
            src_ref=src, dst_ref=dst, send_sem=ss, recv_sem=rsem, device_id=target, device_id_type=MESH
        )

    def signal(sem, target):
        pl.semaphore_signal(sem, inc=1, device_id=target, device_id_type=MESH)

    loads = [
        pltpu.make_async_copy(src, dst, sem_in.at[i])
        for i, (src, dst) in enumerate(
            [
                (q_in, qin), (k_in, kin), (v_in, vin), (g_in, pk.at[G]),
                (stream_in, xs), (weight_in, win), (owner_in, own_ref),
            ]
        )
    ]
    for load in loads:
        load.start()
    xt[...] = jnp.zeros_like(xt)

    plane = []
    for i in range(1, 8):
        p = (me + i) % 8
        plane.append((p // 2, p % 2))
    peers = [dev(yy, z, cc, x) for yy, cc in plane]
    peers += [dev(y, (z + i) % NZ, c, x) for i in (1, NZ - 1)]
    peers += [dev(y, z, c, (x + i) % NX) for i in range(1, NX)]
    barrier = pltpu.get_barrier_semaphore()
    for p in peers:
        signal(barrier, p)

    token = jnp.zeros((CAP, 128), jnp.int32)
    for r in range(CAP):
        token = jnp.where(iota((CAP, 128), 0) == r, chosen_ref[seq * CAP + r] - seq * 128, token)
    pick = (token == iota((CAP, 128), 1)).astype(BF16)
    for load in loads[:4]:
        load.wait()
    pk[Q] = dot(pick, qin[...], 1, 0).astype(BF16)
    pk[K] = dot(pick, kin[...], 1, 0).astype(BF16)
    pk[V] = dot(pick, vin[...], 1, 0).astype(BF16)
    for load in loads[4:]:
        load.wait()
    for t in range(5):
        cols = slice(t * 1024, (t + 1) * 1024)
        xc[:, cols] = dot(pick, xs[:, cols], 1, 0).astype(BF16)
    xc[:, 5120:] = jnp.zeros((CAP, 128), BF16)
    logit = jnp.sum(xc[:, :5120].astype(F32) * win[...].astype(F32), axis=1, keepdims=True)
    spread = jnp.where(
        iota((CAP, 128), 1) == (seq % 8) * CAP + iota((CAP, 128), 0), logit, jnp.zeros((), F32)
    )
    line = jnp.sum(spread, axis=0, keepdims=True)
    ltile[...] = jnp.where(iota((16, 128), 0) == seq // 8, line, jnp.zeros((), F32)).astype(BF16)

    pl.semaphore_wait(barrier, len(peers))

    my_rows = pl.ds(pl.multiple_of(c * CAP, CAP), CAP)

    def to_head(h, cc):
        src = pk.at[2 * cc : 2 * cc + 2, :, pl.ds(h * HD, HD)]
        dst = gat.at[0:2, y, z, my_rows, :] if cc == 0 else ring.at[:, y, z, my_rows, :]
        return remote(src, dst, p1s.at[h, cc], p1r.at[me], dev(h, z, cc, x))

    def to_quarter(cc):
        src = pk.at[2 * cc : 2 * cc + 2, :, pl.ds(4 * HD, HD)]
        dst = quarter.at[:, z, my_rows, :] if cc == 0 else gat.at[2:4, y, z, my_rows, :]
        return remote(src, dst, qr_s, qr_r, dev(y, z, cc, x))

    def to_logit(h):
        return remote(ltile, lplane.at[me], ls.at[h], lr.at[me], dev(h, z, 0, x))

    for h in range(4):
        for cc in range(2):
            here = (c == cc) & (y == h)

            @pl.when(jnp.logical_not(here))
            def _():
                to_head(h, cc).start()

    for h in range(4):

        @pl.when((c != 0) | (y != h))
        def _():
            to_logit(h).start()

    @pl.when(c == 0)
    def _():
        to_quarter(1).start()
        gat[0:2, y, z, my_rows, :] = pk[0:2, :, pl.ds(pl.multiple_of(y * HD, HD), HD)]
        quarter[:, z, my_rows, :] = pk[0:2, :, 4 * HD : 5 * HD]
        lplane[me] = ltile[...]

    @pl.when(c == 1)
    def _():
        to_quarter(0).start()
        ring[:, y, z, my_rows, :] = pk[2:4, :, pl.ds(pl.multiple_of(y * HD, HD), HD)]
        gat[2:4, y, z, my_rows, :] = pk[2:4, :, 4 * HD : 5 * HD]

    for i in range(1, NX):
        signal(xready, dev(y, z, c, (x + i) % NX))

    def piece(cc, a, zz):
        if a == 3:
            return lall.at[zz]
        if a == 2:
            return quarter.at[:, zz] if cc == 0 else gat.at[2:4, y, zz]
        return gat.at[a, :, zz] if cc == 0 else ring.at[a, :, zz]

    def at_distance(s, d):
        return (z - s + 2 * NZ) % NZ if d == 0 else (z + s) % NZ

    def hop(cc, a, s, d, ahead=0):
        ref = piece(cc, a, at_distance(s + ahead, d))
        to = (z + 1) % NZ if d == 0 else (z + NZ - 1) % NZ
        return remote(ref, ref, rs.at[d, a, s], rr.at[d, a, s], dev(y, to, c, x))

    def to_core0(a, zz):
        return remote(ring.at[a, :, zz], gat.at[2 + a, :, zz], ffs.at[a, zz], ffr.at[a, zz], dev(y, z, 0, x))

    def to_head4(cc, zz):
        src = piece(cc, 2, zz)
        return remote(src, gat.at[2 * cc : 2 * cc + 2, y, zz], qfs.at[zz], fr.at[y * 2 + cc, zz], dev(0, z, 1, x))

    def send_quarter(cc, zz):
        if cc == 0:
            to_head4(0, zz).start()
        else:

            @pl.when(y != 0)
            def _():
                to_head4(1, zz).start()

    steps = (8, 7)

    def first_hops(cc):
        for p in range(8):
            yy, pc = p // 2, p % 2
            got = gat.at[0:2, yy, z, pl.ds(pc * CAP, CAP), :] if cc == 0 else ring.at[:, yy, z, pl.ds(pc * CAP, CAP), :]

            @pl.when(p != me)
            def _():
                remote(got, got, p1s.at[0, 0], p1r.at[p], dev(yy, z, pc, x)).wait_recv()

        for a in range(2):
            for d in (0, 1):
                hop(cc, a, 0, d).start()
        if cc == 1:
            to_core0(0, z).start()
            to_core0(1, z).start()
        sib = pl.ds((1 - cc) * CAP, CAP)
        got = quarter.at[:, z, sib, :] if cc == 0 else gat.at[2:4, y, z, sib, :]
        remote(got, got, qr_s, qr_r, dev(y, z, 1 - cc, x)).wait_recv()
        for d in (0, 1):
            hop(cc, 2, 0, d).start()
        send_quarter(cc, z)

    def next_hops(cc, pieces, s):
        for a in range(pieces):
            for d in (0, 1):
                if s - 1 < steps[d]:
                    hop(cc, a, s - 1, d, 1).wait_recv()
                if s < steps[d]:
                    hop(cc, a, s, d).start()
                if s - 1 < steps[d]:
                    if a == 2:
                        send_quarter(cc, at_distance(s, d))
                    if a < 2 and cc == 1:
                        to_core0(a, at_distance(s, d)).start()

    @pl.when(c == 0)
    def _():
        first_hops(0)
        for p in range(8):

            @pl.when(p != me)
            def _():
                remote(ltile, lplane.at[p], ls.at[0], lr.at[p], dev(p // 2, z, p % 2, x)).wait_recv()

        total = jnp.zeros((16, 128), F32)
        for p in range(8):
            total = total + lplane[p].astype(F32)
        lall[z] = total.astype(BF16)
        for d in (0, 1):
            hop(0, 3, 0, d).start()

    @pl.when(c == 1)
    def _():
        first_hops(1)

    sub = iota((128, 128), 0)
    lane = iota((128, 128), 1)

    @pl.when(is_owner)
    def _():
        before = (sub < lane).astype(BF16)
        base = jnp.zeros((128, 1), F32)
        for t in range(16):
            line = own_ref[t : t + 1, :]
            names = (sub == line).astype(F32)
            count = dot(names.astype(BF16), before, 1, 0)
            rank = jnp.sum(names * (count + base), axis=0, keepdims=True)
            base = base + jnp.sum(names, axis=1, keepdims=True)
            slot[t : t + 1, :] = line.astype(F32) * 16.0 + rank
        slot[16:, :] = jnp.zeros((112, 128), F32)

    @pl.when(c == 0)
    def _():
        next_hops(0, 4, 1)

    @pl.when(c == 1)
    def _():
        next_hops(1, 3, 1)

    @pl.when(is_owner)
    def _():
        slot_col = jnp.transpose(slot[...])
        own_slot = ((sub // 32) * 512 + z * 32 + sub % 32).astype(F32)
        for t in range(16):
            cols = slice(t * 128, (t + 1) * 128)
            sel[:, cols] = (own_slot == slot[t : t + 1, :]).astype(BF16)
            column = jnp.broadcast_to(slot_col[:, t : t + 1], (128, 128))
            for u in range(16):
                pt[cols, u * 128 : (u + 1) * 128] = (column == (lane + u * 128).astype(F32)).astype(BF16)

    @pl.when(c == 0)
    def _():
        for s in range(2, 9):
            next_hops(0, 4, s)

    @pl.when(c == 1)
    def _():
        for s in range(2, 9):
            next_hops(1, 3, s)

    def window(zz):
        return pl.ds(pl.multiple_of(x * 1280 + (zz * 80 // 128) * 128, 128), 256)

    xt_rows = pl.ds(pl.multiple_of(z * 32 + c * CAP, CAP), CAP)

    def to_column(i):
        zz = (z + i) % NZ
        return remote(xc.at[:, window(zz)], xt.at[xt_rows, :], xts.at[i], xtr.at[z], dev(y, zz, c, x))

    for i in range(1, NZ):
        to_column(i).start()
    xt[xt_rows, :] = xc[:, window(z)]

    def to_sibling():
        return remote(lsum, lsum, dls, dlr, dev(0, z, 1, x))

    @pl.when(c == 0)
    def _():
        total = jnp.zeros((16, 128), F32)
        for zz in range(NZ):
            total = total + lall[zz].astype(F32)
        lsum[...] = total

        @pl.when(y == 0)
        def _():
            to_sibling().start()

    @pl.when((c == 1) & (y == 0))
    def _():
        to_sibling().wait_recv()
        for yy in range(4):
            for zz in range(NZ):
                ref = gat.at[0:2, yy, zz]
                remote(ref, ref, qfs.at[0], fr.at[yy * 2, zz], dev(yy, z, 0, x)).wait_recv()

    def all_rows(a):
        return gat[a].reshape(ROWS, HD)

    def to_slot_owner(i):
        yy, cc = plane[i - 1]
        theirs = pl.ds(pl.multiple_of(yy * 32 + cc * CAP, CAP), CAP)
        return remote(
            ob.at[:, theirs, :],
            outs.at[:, :, pl.ds(pl.multiple_of(head * HD, HD), HD)],
            outsem_s.at[i], outsem_r.at[head], dev(yy, z, cc, x),
        )

    def to_all(i):
        p = (me + i) % 8
        return remote(
            gl.at[p // 2], lgx.at[mine], gs.at[i], gr.at[mine], dev(p // 2, z, p % 2, (x + i // 8) % NX)
        )

    @pl.when(is_owner)
    def _():
        for t in range(16):
            cols = slice(t * 128, (t + 1) * 128)
            row16 = iota((16, 128), 0)
            lane16 = iota((16, 128), 1)
            value = jnp.where(row16 == 0, t * 8 + lane16 // 16, jnp.where(row16 == 1, lane16 % 16, 0))
            ownx[:, cols] = jnp.where(row16 == 2, lsum[t : t + 1, :], value.astype(F32)).astype(BF16)
            rows[2:3, cols] = jax.nn.sigmoid(lsum[t : t + 1, :])
        own = dot(sel[...], ownx[...], 1, 1)
        own_j = own[:, 0:1] * 16.0 + own[:, 1:2]
        own_j_row = jnp.transpose(jnp.broadcast_to(own_j, (128, 128)))[0:1]
        own_logit_row = jnp.transpose(jnp.broadcast_to(own[:, 2:3], (128, 128)))[0:1]
        own_gate = jax.nn.sigmoid(own_logit_row)

        selw = sel[...]
        q_own = dot(selw, all_rows(Q), 1, 0).astype(BF16)
        k_own = dot(selw, all_rows(K), 1, 0).astype(BF16)

        for t in range(4):
            cols = slice(t * 512, (t + 1) * 512)
            q_block = gat[Q, t].reshape(512, HD)
            most = jnp.full((1, 512), -jnp.inf, F32)
            for u in range(t + 1):
                score = dot(gat[K, u].reshape(512, HD), q_block, 1, 1)
                if u == t:
                    score = jnp.where(iota((512, 512), 0) <= iota((512, 512), 1), score, -jnp.inf)
                st[u * 512 : (u + 1) * 512, :] = score
                most = jnp.maximum(most, jnp.max(score, axis=0, keepdims=True))
            total = jnp.zeros((1, 512), F32)
            for u in range(t + 1):
                keys = slice(u * 512, (u + 1) * 512)
                weight = jnp.exp((st[keys, :] - most) * SCALE)
                total = total + jnp.sum(weight, axis=0, keepdims=True)
                wt[keys, cols] = weight.astype(BF16)
            rows[0:1, cols] = most * SCALE + jnp.log(total)
            rows[3:4, cols] = 1.0 / total

        score = dot(all_rows(K), q_own, 1, 1)
        score = jnp.where(iota((ROWS, 128), 0).astype(F32) <= own_j_row, score, -jnp.inf)
        most = jnp.max(score, axis=0, keepdims=True)
        weight = jnp.exp((score - most) * SCALE)
        wo[...] = (weight * (1.0 / jnp.sum(weight, axis=0, keepdims=True))).astype(BF16)

        score = dot(k_own, all_rows(Q), 1, 1) * SCALE
        causal = iota((128, ROWS), 1).astype(F32) >= own_j
        w2[...] = jnp.exp(jnp.where(causal, score - rows[0:1, :], -jnp.inf)).astype(BF16)

        @pl.when(c == 0)
        def _():
            for zz in range(NZ):
                for a in range(2):
                    to_core0(a, zz).wait_recv()

        @pl.when(c == 1)
        def _():
            for yy in range(1, 4):
                for zz in range(NZ):
                    ref = gat.at[2:4, yy, zz]
                    remote(ref, ref, qfs.at[0], fr.at[yy * 2 + 1, zz], dev(yy, z, 1, x)).wait_recv()

        vt[...] = jnp.transpose(all_rows(V))
        for t in range(4):
            part_rows = slice(t * 512, (t + 1) * 512)
            block = dot(pt[part_rows, :], all_rows(G), 1, 0)
            gc[part_rows, :] = block.astype(BF16)
            gct[:, part_rows] = jnp.transpose(block)
        for t in range(4):
            cols = slice(t * 512, (t + 1) * 512)
            n = (t + 1) * 512
            ctx = dot(vt[:, :n], wt[:n, cols], 1, 0)
            gate_part = jnp.sum(ctx * gct[:, cols], axis=0, keepdims=True) * rows[3:4, cols]
            gating = rows[2:3, cols]
            rows[1:2, cols] = gating * gate_part
            logit_grad = gate_part * gating * (1.0 - gating)
            for u in range(4):
                gl[t, u : u + 1, :] = logit_grad[:, u * 128 : (u + 1) * 128]
            gl[t, 4:8, :] = jnp.zeros((4, 128), F32)
        pl.semaphore_wait(xready, 3)
        for i in range(1, 32):
            to_all(i).start()
        lgx[mine] = gl[y]

        v_own = dot(selw, all_rows(V), 1, 0).astype(BF16)
        g_own = gat[G, :, z].reshape(128, HD)
        ctx = dot(vt[...], wo[...], 1, 0)
        g_own_t = jnp.transpose(g_own.astype(F32))
        delta = jnp.sum(ctx * g_own_t, axis=0, keepdims=True) * own_gate
        ob[0] = jnp.transpose(ctx * own_gate).astype(BF16)
        prob_grad = dot(all_rows(V), g_own, 1, 1) * own_gate
        score_grad = (wo[...].astype(F32) * (prob_grad - delta)).astype(BF16)
        ob[1] = (dot(score_grad, all_rows(K), 0, 0) * SCALE).astype(BF16)

        weight = w2[...].astype(F32)
        prob_grad = dot(v_own, gc[...], 1, 1) * rows[2:3, :]
        score_grad = (weight * (prob_grad - rows[1:2, :])).astype(BF16)
        ob[2] = (dot(score_grad, all_rows(Q), 1, 0) * SCALE).astype(BF16)
        ob[3] = dot((weight * rows[2:3, :]).astype(BF16), gc[...], 1, 0).astype(BF16)
        for i in range(1, 8):
            to_slot_owner(i).start()
        here = pl.ds(pl.multiple_of(y * 32 + c * CAP, CAP), CAP)
        outs[:, :, pl.ds(pl.multiple_of(head * HD, HD), HD)] = ob[:, here, :]

    @pl.when(jnp.logical_not(is_owner))
    def _():
        pl.semaphore_wait(xready, 3)

    for i in range(1, NZ):
        zz = (z + i) % NZ
        got = xt.at[pl.ds(pl.multiple_of(zz * 32 + c * CAP, CAP), CAP), :]
        remote(got, got, xts.at[0], xtr.at[zz], dev(y, zz, c, x)).wait_recv()
    for p in range(20):
        xx, h = p // 5, p % 5
        yy, cc = (h, 0) if h < 4 else (0, 1)

        @pl.when((p != mine) | jnp.logical_not(is_owner))
        def _():
            remote(lgx.at[p], lgx.at[p], gs.at[0], gr.at[p], dev(yy, z, cc, xx)).wait_recv()

    logit_grad = lgx[0]
    for p in range(1, 20):
        logit_grad = logit_grad + lgx[p]
    total = jnp.zeros((8, 256), F32)
    for t in range(4):
        line = jnp.broadcast_to(logit_grad[t : t + 1, :], (8, 128))
        total = total + lax.dot_general(
            line, xt[t * 128 : (t + 1) * 128, :].astype(F32), (((1,), (0,)), ((), ())),
            precision=lax.Precision.HIGHEST, preferred_element_type=F32,
        )
    part[...] = total

    def to_part(xx, cc):
        return remote(part, pr.at[me], prs.at[xx, cc], prr.at[me], dev(x, z, cc, xx))

    def is_me(xx, cc):
        return (y == x) & (x == xx) & (c == cc)

    for xx in range(4):
        for cc in range(2):

            @pl.when(jnp.logical_not(is_me(xx, cc)))
            def _():
                to_part(xx, cc).start()

    @pl.when(y == x)
    def _():
        pr[me] = part[...]

    for p in range(8):

        @pl.when((p != me) | (y != x))
        def _():
            remote(pr.at[p], pr.at[p], prs.at[0, 0], prr.at[p], dev(p // 2, z, p % 2, y)).wait_recv()

    total = pr[0]
    for p in range(1, 8):
        total = total + pr[p]
    offset = (z * 80) % 128 + c * 40
    router_ref[...] = pltpu.roll(total, (256 - offset) % 256, 1)[:, :128]

    for h in range(5):
        yy, cc = (h, 0) if h < 4 else (0, 1)

        @pl.when((yy != y) | (cc != c))
        def _():
            got = outs.at[:, :, pl.ds(h * HD, HD)]
            remote(got, got, outsem_s.at[0], outsem_r.at[h], dev(yy, z, cc, x)).wait_recv()

    out_ref[...] = outs[...]

    for h in range(4):
        for cc in range(2):

            @pl.when((c != cc) | (y != h))
            def _():
                to_head(h, cc).wait_send()

        @pl.when((c != 0) | (y != h))
        def _():
            to_logit(h).wait_send()

    @pl.when(c == 0)
    def _():
        to_quarter(1).wait_send()
        for s in range(8):
            for a in range(4):
                for d in (0, 1):
                    if s < steps[d]:
                        hop(0, a, s, d).wait_send()
        for zz in range(NZ):
            to_head4(0, zz).wait_send()

        @pl.when(y == 0)
        def _():
            to_sibling().wait_send()

    @pl.when(c == 1)
    def _():
        to_quarter(0).wait_send()
        for s in range(8):
            for a in range(3):
                for d in (0, 1):
                    if s < steps[d]:
                        hop(1, a, s, d).wait_send()
        for zz in range(NZ):
            to_core0(0, zz).wait_send()
            to_core0(1, zz).wait_send()

        @pl.when(y != 0)
        def _():
            for zz in range(NZ):
                to_head4(1, zz).wait_send()

    for i in range(1, NZ):
        to_column(i).wait_send()

    @pl.when(is_owner)
    def _():
        for i in range(1, 8):
            to_slot_owner(i).wait_send()
        for i in range(1, 32):
            to_all(i).wait_send()

    for xx in range(4):
        for cc in range(2):

            @pl.when(jnp.logical_not(is_me(xx, cc)))
            def _():
                to_part(xx, cc).wait_send()


def body(stream, queries, keys, values, router_weight, chosen, owner, grad_out):
    vmem = pl.BlockSpec(memory_space=pltpu.VMEM)
    hbm = pl.BlockSpec(memory_space=pl.ANY)
    dma = pltpu.SemaphoreType.DMA
    scratch = [
        pltpu.VMEM((128, 5120), BF16),
        pltpu.VMEM((128, 5 * HD), BF16),
        pltpu.VMEM((128, 5 * HD), BF16),
        pltpu.VMEM((128, 5 * HD), BF16),
        pltpu.VMEM((1, 5120), BF16),
        pltpu.VMEM((16, 128), jnp.int32),
        pltpu.VMEM((4, CAP, 5 * HD), BF16),
        pltpu.VMEM((4, NY, NZ, 32, HD), BF16),
        pltpu.VMEM((2, NY, NZ, 32, HD), BF16),
        pltpu.VMEM((2, NZ, 32, HD), BF16),
        pltpu.VMEM((CAP, 5248), BF16),
        pltpu.VMEM((512, 256), BF16),
        pltpu.VMEM((16, 128), BF16),
        pltpu.VMEM((8, 16, 128), BF16),
        pltpu.VMEM((NZ, 16, 128), BF16),
        pltpu.VMEM((16, 128), F32),
        pltpu.VMEM((128, 128), F32),
        pltpu.VMEM((ROWS, ROWS), BF16),
        pltpu.VMEM((128, ROWS), BF16),
        pltpu.VMEM((16, ROWS), BF16),
        pltpu.VMEM((ROWS, 512), F32),
        pltpu.VMEM((ROWS, ROWS), BF16),
        pltpu.VMEM((ROWS, 128), BF16),
        pltpu.VMEM((128, ROWS), BF16),
        pltpu.VMEM((HD, ROWS), BF16),
        pltpu.VMEM((HD, ROWS), F32),
        pltpu.VMEM((ROWS, HD), BF16),
        pltpu.VMEM((8, ROWS), F32),
        pltpu.VMEM((4, 128, HD), BF16),
        pltpu.VMEM((4, CAP, 5 * HD), BF16),
        pltpu.VMEM((NY, 8, 128), F32),
        pltpu.VMEM((20, 8, 128), F32),
        pltpu.VMEM((8, 256), F32),
        pltpu.VMEM((8, 8, 256), F32),
        dma((7,)), dma((4, 2)), dma((8,)), dma, dma, dma((4,)), dma((8,)),
        dma((2, 4, 8)), dma((2, 4, 8)), dma((2, 16)), dma((2, 16)), dma((16,)), dma((8, 16)), dma, dma,
        dma((16,)), dma((16,)), dma((8,)), dma((5,)), dma((32,)), dma((20,)), dma((4, 2)), dma((8,)),
        pltpu.SemaphoreType.REGULAR,
    ]
    out, router = pl.pallas_call(
        kernel,
        out_shape=(
            jax.ShapeDtypeStruct((4, CAP, 5 * HD), BF16),
            jax.ShapeDtypeStruct((8, 128), F32),
        ),
        in_specs=[pl.BlockSpec(memory_space=pltpu.SMEM)] + [hbm] * 7,
        out_specs=(vmem,) * 2,
        scratch_shapes=scratch,
        compiler_params=pltpu.CompilerParams(
            collective_id=0, has_side_effects=True, vmem_limit_bytes=56 * 2**20
        ),
        name="routed_attention",
    )(
        chosen, owner.reshape(16, 128), router_weight.reshape(1, -1),
        queries, keys, values, grad_out, stream,
    )

    def split(out_ref, router_in, *refs):
        for i in range(4):
            refs[i][...] = out_ref[i]
        refs[4][...] = router_in[...]

    wide = jax.ShapeDtypeStruct((CAP, 5 * HD), BF16)
    *big, router = pl.pallas_call(
        split,
        out_shape=(wide, wide, wide, wide, jax.ShapeDtypeStruct((8, 128), F32)),
        in_specs=[vmem] * 2,
        out_specs=(vmem,) * 5,
        name="split_outputs",
    )(out, router)
    return (*big, router[0, :40])


def solution(mesh):
    return jax.shard_map(
        body,
        mesh=mesh,
        in_specs=(
            P("seq", None),
            P("seq", "head"),
            P("seq", "head"),
            P("seq", "head"),
            P(),
            P(),
            P(),
            P("seq", "head"),
        ),
        out_specs=(
            P("seq", "head"),
            P("seq", "head"),
            P("seq", "head"),
            P("seq", "head"),
            P("seq"),
        ),
        check_vma=False,
    )
```

time: 86.3 us -> 77.5 us (0.90)
  local copies, waits for them, and re-layouts: 9.83 us -> 2.5 us
    unnamed x18 -> x0, local copies, waits for them, and re-layouts: 8.6 us -> none
    pallas_call x1 -> x2, Pallas kernels: 74.8 us -> 74 us  [the longest x1 72.5 us: body(): pl.pallas_call(kernel, out_shape=(jax.ShapeDtypeStruct((4, CAP, 5 * HD),...]
where the time goes in v2:
time: 77.5 us; the launch traced here: 77.2 us
  Pallas kernels  74 us (95%)
  local copies, waits for them, and re-layouts  2.5 us (3%)
    pallas_call x1, Pallas kernels, body(): pl.pallas_call(kernel, out_shape=(jax.ShapeDtypeStruct((4, CAP, 5 * HD),...  72.5 us

profile of v2, /device:TPU:1, one launch (start us, length us, event | category | flops | bytes accessed | tf_op | source)
XLA Modules:
  0.0 77.2 jit_solution(15885886519793421427)
XLA Ops:
  0.6 1.3 %reshape.17.weight_in = bf16[1,5120]{1,0:T(2,128)(2,1)} reshape(bf16[5120]{0:T(1024)(128)(2,1)} %param.12) | data formatting | bytes 20480 | tf_op jit(solution)/shard_map/reshape | solution.py:621
  2.0 72.5 %routed_attention.1 = (bf16[4,16,640]{2,1,0:T(8,128)(2,1)}, f32[8,128]{1,0:T(8,128)}) custom-call(s32[2048]{0:T(1024)} %chosen_ref.1, s32[16,128]{1,0:T(8,128)} %bitcast.3, bf16[1,5120]{1,0:T(2,128)(2,1)} %reshape.17.weight_in, bf16[128,640]{1,0:T(8,128)(2,1)} %q_in.1, bf16[128,640]{1,0:T(8,128)(2,1)} %k_in.1, bf16[128,640]{1,0:T(8,128)(2,1)} %v_in.1, ...), custom_call_target="tpu_custom_call" | custom-call | tf_op jit(solution)/shard_map/routed_attention/pallas_call | solution.py:607
  74.5 1.5 %split_outputs.1 = (bf16[16,640]{1,0:T(8,128)(2,1)}, bf16[16,640]{1,0:T(8,128)(2,1)}, bf16[16,640]{1,0:T(8,128)(2,1)}, bf16[16,640]{1,0:T(8,128)(2,1)}, f32[8,128]{1,0:T(8,128)}) custom-call(bf16[4,16,640]{2,1,0:T(8,128)(2,1)} %get-tuple-element.12.out_ref, f32[8,128]{1,0:T(8,128)} %get-tuple-element.13.router_in), custom_call_target="tpu_custom_call" | custom-call | tf_op jit(solution)/shard_map/split_outputs/pallas_call | solution.py:631
  76.0 1.2 %slice_bitcast_fusion = f32[40]{0:T(128)} fusion(f32[8,128]{1,0:T(8,128)} %get-tuple-element.18), kind=kLoop, calls=%fused_computation | loop fusion | bytes 320 | tf_op jit(solution)/shard_map/squeeze | solution.py:638

commit v3 on v2

--- a/solution.py
+++ b/solution.py
@@ -26,7 +26,7 @@
 def kernel(
     chosen_ref, owner_in, weight_in, q_in, k_in, v_in, g_in, stream_in,
     out_ref, router_ref,
-    xs, qin, kin, vin, win, own_ref, pk, gat, ring, quarter, xc, xt, ltile, lplane, lall, lsum,
+    xs, qin, kin, vin, win, own_ref, pk, gat, ring, xc, xt, ltile, lplane, lall, lsum,
     slot, pt, sel, ownx, st, wt, wo, w2, vt, gct, gc, rows, ob, outs,
     gl, lgx, part, pr,
     sem_in, p1s, p1r, qr_s, qr_r, ls, lr, rs, rr, ffs, ffr, qfs, fr, dls, dlr, xts, xtr,
@@ -68,7 +68,7 @@
         p = (me + i) % 8
         plane.append((p // 2, p % 2))
     peers = [dev(yy, z, cc, x) for yy, cc in plane]
-    peers += [dev(y, (z + i) % NZ, c, x) for i in (1, NZ - 1)]
+    peers += [dev(y, (z + i) % NZ, c, x) for i in (1, NZ - 1, 4, NZ - 4)]
     peers += [dev(y, z, c, (x + i) % NX) for i in range(1, NX)]
     barrier = pltpu.get_barrier_semaphore()
     for p in peers:
@@ -83,45 +83,54 @@
     pk[Q] = dot(pick, qin[...], 1, 0).astype(BF16)
     pk[K] = dot(pick, kin[...], 1, 0).astype(BF16)
     pk[V] = dot(pick, vin[...], 1, 0).astype(BF16)
+    pl.semaphore_wait(barrier, len(peers))
+
+    my_rows = pl.ds(pl.multiple_of(c * CAP, CAP), CAP)
+
+    def to_head(h, cc):
+        src = pk.at[2 - 2 * cc : 4 - 2 * cc, :, pl.ds(h * HD, HD)]
+        dst = gat.at[2:4, y, z, my_rows, :] if cc == 0 else ring.at[:, y, z, my_rows, :]
+        return remote(src, dst, p1s.at[h, cc], p1r.at[me], dev(h, z, cc, x))
+
+    def to_quarter():
+        src = pk.at[:, :, pl.ds(4 * HD, HD)]
+        return remote(src, gat.at[:, y, z, my_rows, :], qr_s, qr_r, dev(y, z, 1, x))
+
+    def to_logit(h):
+        return remote(ltile, lplane.at[me], ls.at[h], lr.at[me], dev(h, z, 0, x))
+
+    for h in range(4):
+        for cc in range(2):
+            here = (c == cc) & (y == h)
+
+            @pl.when(jnp.logical_not(here))
+            def _():
+                to_head(h, cc).start()
+
+    @pl.when(c == 0)
+    def _():
+        to_quarter().start()
+        gat[2:4, y, z, my_rows, :] = pk[2:4, :, pl.ds(pl.multiple_of(y * HD, HD), HD)]
+
+    @pl.when(c == 1)
+    def _():
+        ring[:, y, z, my_rows, :] = pk[0:2, :, pl.ds(pl.multiple_of(y * HD, HD), HD)]
+        gat[:, y, z, my_rows, :] = pk[:, :, 4 * HD : 5 * HD]
+
     for load in loads[4:]:
         load.wait()
     for t in range(5):
         cols = slice(t * 1024, (t + 1) * 1024)
         xc[:, cols] = dot(pick, xs[:, cols], 1, 0).astype(BF16)
     xc[:, 5120:] = jnp.zeros((CAP, 128), BF16)
-    logit = jnp.sum(xc[:, :5120].astype(F32) * win[...].astype(F32), axis=1, keepdims=True)
+    logit = jnp.sum(xc[:, :5120].astype(F32) * win[...].reshape(1, 5120).astype(F32), axis=1, keepdims=True)
     spread = jnp.where(
         iota((CAP, 128), 1) == (seq % 8) * CAP + iota((CAP, 128), 0), logit, jnp.zeros((), F32)
     )
     line = jnp.sum(spread, axis=0, keepdims=True)
     ltile[...] = jnp.where(iota((16, 128), 0) == seq // 8, line, jnp.zeros((), F32)).astype(BF16)
 
-    pl.semaphore_wait(barrier, len(peers))
-
-    my_rows = pl.ds(pl.multiple_of(c * CAP, CAP), CAP)
-
-    def to_head(h, cc):
-        src = pk.at[2 * cc : 2 * cc + 2, :, pl.ds(h * HD, HD)]
-        dst = gat.at[0:2, y, z, my_rows, :] if cc == 0 else ring.at[:, y, z, my_rows, :]
-        return remote(src, dst, p1s.at[h, cc], p1r.at[me], dev(h, z, cc, x))
-
-    def to_quarter(cc):
-        src = pk.at[2 * cc : 2 * cc + 2, :, pl.ds(4 * HD, HD)]
-        dst = quarter.at[:, z, my_rows, :] if cc == 0 else gat.at[2:4, y, z, my_rows, :]
-        return remote(src, dst, qr_s, qr_r, dev(y, z, cc, x))
-
-    def to_logit(h):
-        return remote(ltile, lplane.at[me], ls.at[h], lr.at[me], dev(h, z, 0, x))
-
     for h in range(4):
-        for cc in range(2):
-            here = (c == cc) & (y == h)
-
-            @pl.when(jnp.logical_not(here))
-            def _():
-                to_head(h, cc).start()
-
-    for h in range(4):
 
         @pl.when((c != 0) | (y != h))
         def _():
@@ -129,87 +138,92 @@
 
     @pl.when(c == 0)
     def _():
-        to_quarter(1).start()
-        gat[0:2, y, z, my_rows, :] = pk[0:2, :, pl.ds(pl.multiple_of(y * HD, HD), HD)]
-        quarter[:, z, my_rows, :] = pk[0:2, :, 4 * HD : 5 * HD]
         lplane[me] = ltile[...]
-
-    @pl.when(c == 1)
-    def _():
-        to_quarter(0).start()
-        ring[:, y, z, my_rows, :] = pk[2:4, :, pl.ds(pl.multiple_of(y * HD, HD), HD)]
-        gat[2:4, y, z, my_rows, :] = pk[2:4, :, 4 * HD : 5 * HD]
 
     for i in range(1, NX):
         signal(xready, dev(y, z, c, (x + i) % NX))
 
+    paths = (
+        (((0, 1), (0, 4)), ((1, 2), (4, 5)), ((2, 3), (5, 6)), ((6, 7),), ((7, 8),)),
+        (((0, 1),), ((1, 2),), ((2, 3),), ((3, 4),), ((4, 5),), ((5, 6),), ((6, 7),), ((7, 8),)),
+    )
+    most_far = (8, 7)
+    pieces = (3, 4)
+
     def piece(cc, a, zz):
-        if a == 3:
-            return lall.at[zz]
-        if a == 2:
-            return quarter.at[:, zz] if cc == 0 else gat.at[2:4, y, zz]
-        return gat.at[a, :, zz] if cc == 0 else ring.at[a, :, zz]
+        if cc == 0:
+            return lall.at[zz] if a == 2 else gat.at[2 + a, :, zz]
+        return gat.at[0:2, y, zz] if a == 0 else gat.at[2:4, y, zz] if a == 3 else ring.at[a - 1, :, zz]
 
     def at_distance(s, d):
         return (z - s + 2 * NZ) % NZ if d == 0 else (z + s) % NZ
 
-    def hop(cc, a, s, d, ahead=0):
-        ref = piece(cc, a, at_distance(s + ahead, d))
-        to = (z + 1) % NZ if d == 0 else (z + NZ - 1) % NZ
-        return remote(ref, ref, rs.at[d, a, s], rr.at[d, a, s], dev(y, to, c, x))
+    def hop(cc, a, near, far, d):
+        ref = piece(cc, a, at_distance(near, d))
+        to = (z + far - near) % NZ if d == 0 else (z + near - far + NZ) % NZ
+        return remote(ref, ref, rs.at[d, a, far], rr.at[d, a, far], dev(y, to, c, x))
+
+    def arrival(cc, a, far, d):
+        ref = piece(cc, a, at_distance(far, d))
+        return remote(ref, ref, rs.at[d, a, far], rr.at[d, a, far], dev(y, z, c, x))
 
     def to_core0(a, zz):
-        return remote(ring.at[a, :, zz], gat.at[2 + a, :, zz], ffs.at[a, zz], ffr.at[a, zz], dev(y, z, 0, x))
-
-    def to_head4(cc, zz):
-        src = piece(cc, 2, zz)
-        return remote(src, gat.at[2 * cc : 2 * cc + 2, y, zz], qfs.at[zz], fr.at[y * 2 + cc, zz], dev(0, z, 1, x))
-
-    def send_quarter(cc, zz):
-        if cc == 0:
-            to_head4(0, zz).start()
+        return remote(ring.at[a, :, zz], gat.at[a, :, zz], ffs.at[a, zz], ffr.at[a, zz], dev(y, z, 0, x))
+
+    def to_head4(b, zz):
+        ref = gat.at[2 * b : 2 * b + 2, y, zz]
+        return remote(ref, ref, qfs.at[b, zz], fr.at[b, y, zz], dev(0, z, 1, x))
+
+    def pass_on(a, zz):
+        if a in (0, 3):
+
+            @pl.when(y != 0)
+            def _():
+                to_head4(a // 3, zz).start()
         else:
-
-            @pl.when(y != 0)
-            def _():
-                to_head4(1, zz).start()
-
-    steps = (8, 7)
+            to_core0(a - 1, zz).start()
+
+    def hops(cc, a, level):
+        for near, far in paths[cc][level]:
+            for d in (0, 1):
+                if near > 0:
+                    arrival(cc, a, near, d).wait_recv()
+                if far <= most_far[d]:
+                    hop(cc, a, near, far, d).start()
+                if cc == 1:
+                    pass_on(a, at_distance(near, d)) if near > 0 or (d == 0 and far == 1) else None
+
+    def all_hops(cc, levels):
+        for level in levels:
+            for a in range(pieces[cc]):
+                hops(cc, a, level)
+
+    def last_arrivals(cc):
+        starts = [near for level in paths[cc] for near, _ in level]
+        for a in range(pieces[cc]):
+            for far in range(1, 9):
+                for d in (0, 1):
+                    if far not in starts and far <= most_far[d]:
+                        arrival(cc, a, far, d).wait_recv()
+                        if cc == 1:
+                            pass_on(a, at_distance(far, d))
 
     def first_hops(cc):
         for p in range(8):
             yy, pc = p // 2, p % 2
-            got = gat.at[0:2, yy, z, pl.ds(pc * CAP, CAP), :] if cc == 0 else ring.at[:, yy, z, pl.ds(pc * CAP, CAP), :]
+            got = gat.at[2:4, yy, z, pl.ds(pc * CAP, CAP), :] if cc == 0 else ring.at[:, yy, z, pl.ds(pc * CAP, CAP), :]
 
             @pl.when(p != me)
             def _():
                 remote(got, got, p1s.at[0, 0], p1r.at[p], dev(yy, z, pc, x)).wait_recv()
 
-        for a in range(2):
-            for d in (0, 1):
-                hop(cc, a, 0, d).start()
         if cc == 1:
-            to_core0(0, z).start()
-            to_core0(1, z).start()
-        sib = pl.ds((1 - cc) * CAP, CAP)
-        got = quarter.at[:, z, sib, :] if cc == 0 else gat.at[2:4, y, z, sib, :]
-        remote(got, got, qr_s, qr_r, dev(y, z, 1 - cc, x)).wait_recv()
-        for d in (0, 1):
-            hop(cc, 2, 0, d).start()
-        send_quarter(cc, z)
-
-    def next_hops(cc, pieces, s):
-        for a in range(pieces):
-            for d in (0, 1):
-                if s - 1 < steps[d]:
-                    hop(cc, a, s - 1, d, 1).wait_recv()
-                if s < steps[d]:
-                    hop(cc, a, s, d).start()
-                if s - 1 < steps[d]:
-                    if a == 2:
-                        send_quarter(cc, at_distance(s, d))
-                    if a < 2 and cc == 1:
-                        to_core0(a, at_distance(s, d)).start()
+            got = gat.at[:, y, z, pl.ds(0, CAP), :]
+            remote(got, got, qr_s, qr_r, dev(y, z, 0, x)).wait_recv()
+            all_hops(1, (0,))
+        else:
+            hops(0, 0, 0)
+            hops(0, 1, 0)
 
     @pl.when(c == 0)
     def _():
@@ -224,8 +238,7 @@
         for p in range(8):
             total = total + lplane[p].astype(F32)
         lall[z] = total.astype(BF16)
-        for d in (0, 1):
-            hop(0, 3, 0, d).start()
+        hops(0, 2, 0)
 
     @pl.when(c == 1)
     def _():
@@ -249,11 +262,11 @@
 
     @pl.when(c == 0)
     def _():
-        next_hops(0, 4, 1)
+        all_hops(0, (1,))
 
     @pl.when(c == 1)
     def _():
-        next_hops(1, 3, 1)
+        all_hops(1, (1,))
 
     @pl.when(is_owner)
     def _():
@@ -268,13 +281,12 @@
 
     @pl.when(c == 0)
     def _():
-        for s in range(2, 9):
-            next_hops(0, 4, s)
+        all_hops(0, range(2, len(paths[0])))
 
     @pl.when(c == 1)
     def _():
-        for s in range(2, 9):
-            next_hops(1, 3, s)
+        all_hops(1, range(2, len(paths[1])))
+        last_arrivals(1)
 
     def window(zz):
         return pl.ds(pl.multiple_of(x * 1280 + (zz * 80 // 128) * 128, 128), 256)
@@ -285,31 +297,23 @@
         zz = (z + i) % NZ
         return remote(xc.at[:, window(zz)], xt.at[xt_rows, :], xts.at[i], xtr.at[z], dev(y, zz, c, x))
 
-    for i in range(1, NZ):
-        to_column(i).start()
+    late = (3, 8, 13)
+
+    @pl.when(c == 0)
+    def _():
+        for i in range(1, NZ):
+            if i not in late:
+                to_column(i).start()
+
+    @pl.when(c == 1)
+    def _():
+        for i in range(1, NZ):
+            to_column(i).start()
+
     xt[xt_rows, :] = xc[:, window(z)]
 
     def to_sibling():
         return remote(lsum, lsum, dls, dlr, dev(0, z, 1, x))
-
-    @pl.when(c == 0)
-    def _():
-        total = jnp.zeros((16, 128), F32)
-        for zz in range(NZ):
-            total = total + lall[zz].astype(F32)
-        lsum[...] = total
-
-        @pl.when(y == 0)
-        def _():
-            to_sibling().start()
-
-    @pl.when((c == 1) & (y == 0))
-    def _():
-        to_sibling().wait_recv()
-        for yy in range(4):
-            for zz in range(NZ):
-                ref = gat.at[0:2, yy, zz]
-                remote(ref, ref, qfs.at[0], fr.at[yy * 2, zz], dev(yy, z, 0, x)).wait_recv()
 
     def all_rows(a):
         return gat[a].reshape(ROWS, HD)
@@ -331,18 +335,28 @@
 
     @pl.when(is_owner)
     def _():
+        @pl.when(c == 0)
+        def _():
+            for zz in range(NZ):
+                for a in range(2):
+                    to_core0(a, zz).wait_recv()
+
+        @pl.when(c == 1)
+        def _():
+            for yy in range(1, 4):
+                for zz in range(NZ):
+                    ref = gat.at[0:2, yy, zz]
+                    remote(ref, ref, qfs.at[0, 0], fr.at[0, yy, zz], dev(yy, z, 1, x)).wait_recv()
+
         for t in range(16):
             cols = slice(t * 128, (t + 1) * 128)
             row16 = iota((16, 128), 0)
             lane16 = iota((16, 128), 1)
             value = jnp.where(row16 == 0, t * 8 + lane16 // 16, jnp.where(row16 == 1, lane16 % 16, 0))
-            ownx[:, cols] = jnp.where(row16 == 2, lsum[t : t + 1, :], value.astype(F32)).astype(BF16)
-            rows[2:3, cols] = jax.nn.sigmoid(lsum[t : t + 1, :])
+            ownx[:, cols] = value.astype(F32).astype(BF16)
         own = dot(sel[...], ownx[...], 1, 1)
         own_j = own[:, 0:1] * 16.0 + own[:, 1:2]
         own_j_row = jnp.transpose(jnp.broadcast_to(own_j, (128, 128)))[0:1]
-        own_logit_row = jnp.transpose(jnp.broadcast_to(own[:, 2:3], (128, 128)))[0:1]
-        own_gate = jax.nn.sigmoid(own_logit_row)
 
         selw = sel[...]
         q_own = dot(selw, all_rows(Q), 1, 0).astype(BF16)
@@ -379,16 +393,30 @@
 
         @pl.when(c == 0)
         def _():
+            last_arrivals(0)
+            for i in late:
+                to_column(i).start()
+            total = jnp.zeros((16, 128), F32)
             for zz in range(NZ):
-                for a in range(2):
-                    to_core0(a, zz).wait_recv()
+                total = total + lall[zz].astype(F32)
+            lsum[...] = total
+
+            @pl.when(y == 0)
+            def _():
+                to_sibling().start()
 
         @pl.when(c == 1)
         def _():
+            to_sibling().wait_recv()
             for yy in range(1, 4):
                 for zz in range(NZ):
                     ref = gat.at[2:4, yy, zz]
-                    remote(ref, ref, qfs.at[0], fr.at[yy * 2 + 1, zz], dev(yy, z, 1, x)).wait_recv()
+                    remote(ref, ref, qfs.at[0, 0], fr.at[1, yy, zz], dev(yy, z, 1, x)).wait_recv()
+
+        for t in range(16):
+            cols = slice(t * 128, (t + 1) * 128)
+            ownx[:, cols] = jnp.broadcast_to(lsum[t : t + 1, :], (16, 128)).astype(BF16)
+            rows[2:3, cols] = jax.nn.sigmoid(lsum[t : t + 1, :])
 
         vt[...] = jnp.transpose(all_rows(V))
         for t in range(4):
@@ -412,6 +440,8 @@
             to_all(i).start()
         lgx[mine] = gl[y]
 
+        own = dot(sel[...], ownx[...], 1, 1)
+        own_gate = jax.nn.sigmoid(jnp.transpose(jnp.broadcast_to(own[:, 0:1], (128, 128)))[0:1])
         v_own = dot(selw, all_rows(V), 1, 0).astype(BF16)
         g_own = gat[G, :, z].reshape(128, HD)
         ctx = dot(vt[...], wo[...], 1, 0)
@@ -510,16 +540,18 @@
         def _():
             to_logit(h).wait_send()
 
+    def sent(cc):
+        for a in range(pieces[cc]):
+            for level in paths[cc]:
+                for near, far in level:
+                    for d in (0, 1):
+                        if far <= most_far[d]:
+                            hop(cc, a, near, far, d).wait_send()
+
     @pl.when(c == 0)
     def _():
-        to_quarter(1).wait_send()
-        for s in range(8):
-            for a in range(4):
-                for d in (0, 1):
-                    if s < steps[d]:
-                        hop(0, a, s, d).wait_send()
-        for zz in range(NZ):
-            to_head4(0, zz).wait_send()
+        to_quarter().wait_send()
+        sent(0)
 
         @pl.when(y == 0)
         def _():
@@ -527,12 +559,7 @@
 
     @pl.when(c == 1)
     def _():
-        to_quarter(0).wait_send()
-        for s in range(8):
-            for a in range(3):
-                for d in (0, 1):
-                    if s < steps[d]:
-                        hop(1, a, s, d).wait_send()
+        sent(1)
         for zz in range(NZ):
             to_core0(0, zz).wait_send()
             to_core0(1, zz).wait_send()
@@ -540,6 +567,7 @@
         @pl.when(y != 0)
         def _():
             for zz in range(NZ):
+                to_head4(0, zz).wait_send()
                 to_head4(1, zz).wait_send()
 
     for i in range(1, NZ):
@@ -569,12 +597,11 @@
         pltpu.VMEM((128, 5 * HD), BF16),
         pltpu.VMEM((128, 5 * HD), BF16),
         pltpu.VMEM((128, 5 * HD), BF16),
-        pltpu.VMEM((1, 5120), BF16),
+        pltpu.VMEM((5120,), BF16),
         pltpu.VMEM((16, 128), jnp.int32),
         pltpu.VMEM((4, CAP, 5 * HD), BF16),
         pltpu.VMEM((4, NY, NZ, 32, HD), BF16),
         pltpu.VMEM((2, NY, NZ, 32, HD), BF16),
-        pltpu.VMEM((2, NZ, 32, HD), BF16),
         pltpu.VMEM((CAP, 5248), BF16),
         pltpu.VMEM((512, 256), BF16),
         pltpu.VMEM((16, 128), BF16),
@@ -600,7 +627,7 @@
         pltpu.VMEM((8, 256), F32),
         pltpu.VMEM((8, 8, 256), F32),
         dma((7,)), dma((4, 2)), dma((8,)), dma, dma, dma((4,)), dma((8,)),
-        dma((2, 4, 8)), dma((2, 4, 8)), dma((2, 16)), dma((2, 16)), dma((16,)), dma((8, 16)), dma, dma,
+        dma((2, 4, 9)), dma((2, 4, 9)), dma((2, 16)), dma((2, 16)), dma((2, 16)), dma((2, 4, 16)), dma, dma,
         dma((16,)), dma((16,)), dma((8,)), dma((5,)), dma((32,)), dma((20,)), dma((4, 2)), dma((8,)),
         pltpu.SemaphoreType.REGULAR,
     ]
@@ -618,24 +645,23 @@
         ),
         name="routed_attention",
     )(
-        chosen, owner.reshape(16, 128), router_weight.reshape(1, -1),
+        chosen, owner.reshape(16, 128), router_weight,
         queries, keys, values, grad_out, stream,
     )
 
     def split(out_ref, router_in, *refs):
         for i in range(4):
             refs[i][...] = out_ref[i]
-        refs[4][...] = router_in[...]
+        refs[4][...] = router_in[0, :40]
 
     wide = jax.ShapeDtypeStruct((CAP, 5 * HD), BF16)
-    *big, router = pl.pallas_call(
+    return pl.pallas_call(
         split,
-        out_shape=(wide, wide, wide, wide, jax.ShapeDtypeStruct((8, 128), F32)),
+        out_shape=(wide, wide, wide, wide, jax.ShapeDtypeStruct((40,), F32)),
         in_specs=[vmem] * 2,
         out_specs=(vmem,) * 5,
         name="split_outputs",
     )(out, router)
-    return (*big, router[0, :40])
 
 
 def solution(mesh):

time: 77.5 us -> 70 us (0.903)
  Pallas kernels: 74 us -> 69.2 us
  local copies, waits for them, and re-layouts: 2.5 us -> 0 us
    pallas_call x1, Pallas kernels: 72.5 us -> 67.6 us  [body(): pl.pallas_call(kernel, out_shape=(jax.ShapeDtypeStruct((4, CAP, 5 * HD),...]
    reshape x1 -> x0, local copies, waits for them, and re-layouts: 1.32 us -> none  [body(): router_weight.reshape(1, -1)]
    squeeze x1 -> x0, local copies, waits for them, and re-layouts: 1.18 us -> none  [body(): return (*big, router[0, :40])]
where the time goes in v3:
time: 70 us; the launch traced here: 69.8 us
  Pallas kernels  69.2 us (99%)
    pallas_call x1, Pallas kernels, body(): pl.pallas_call(kernel, out_shape=(jax.ShapeDtypeStruct((4, CAP, 5 * HD),...  67.6 us
    pallas_call x1, Pallas kernels, body(): pl.pallas_call(split, out_shape=(wide, wide, wide, wide, jax.ShapeDtypeSt...  1.52 us

profile of v3, /device:TPU:1, one launch (start us, length us, event | category | flops | bytes accessed | tf_op | source)
XLA Modules:
  0.0 69.8 jit_solution(12032171408154528517)
XLA Ops:
  0.6 67.6 %routed_attention.1 = (bf16[4,16,640]{2,1,0:T(8,128)(2,1)}, f32[8,128]{1,0:T(8,128)}) custom-call(s32[2048]{0:T(1024)} %chosen_ref.1, s32[16,128]{1,0:T(8,128)} %bitcast.1, bf16[5120]{0:T(1024)(128)(2,1)} %weight_in.1, bf16[128,640]{1,0:T(8,128)(2,1)} %q_in.1, bf16[128,640]{1,0:T(8,128)(2,1)} %k_in.1, bf16[128,640]{1,0:T(8,128)(2,1)} %v_in.1, ...), custom_call_target="tpu_custom_call" | custom-call | tf_op jit(solution)/shard_map/routed_attention/pallas_call | solution.py:634
  68.3 1.5 %split_outputs.1 = (bf16[16,640]{1,0:T(8,128)(2,1)}, bf16[16,640]{1,0:T(8,128)(2,1)}, bf16[16,640]{1,0:T(8,128)(2,1)}, bf16[16,640]{1,0:T(8,128)(2,1)}, f32[40]{0:T(128)}) custom-call(bf16[4,16,640]{2,1,0:T(8,128)(2,1)} %get-tuple-element.7.out_ref, f32[8,128]{1,0:T(8,128)} %get-tuple-element.8.router_in), custom_call_target="tpu_custom_call" | custom-call | tf_op jit(solution)/shard_map/split_outputs/pallas_call | solution.py:658

commit v4 on v3

--- a/solution.py
+++ b/solution.py
@@ -10,6 +10,7 @@
 HD = 128
 ROWS = 2048
 SCALE = HD**-0.5
+SCALE2 = SCALE * 1.4426950408889634
 MESH = pl.DeviceIdType.MESH
 Q, K, G, V = 0, 1, 2, 3
 F32, BF16 = jnp.float32, jnp.bfloat16
@@ -59,9 +60,8 @@
             ]
         )
     ]
-    for load in loads:
+    for load in loads[:4]:
         load.start()
-    xt[...] = jnp.zeros_like(xt)
 
     plane = []
     for i in range(1, 8):
@@ -73,6 +73,8 @@
     barrier = pltpu.get_barrier_semaphore()
     for p in peers:
         signal(barrier, p)
+    for load in loads[4:]:
+        load.start()
 
     token = jnp.zeros((CAP, 128), jnp.int32)
     for r in range(CAP):
@@ -295,7 +297,7 @@
 
     def to_column(i):
         zz = (z + i) % NZ
-        return remote(xc.at[:, window(zz)], xt.at[xt_rows, :], xts.at[i], xtr.at[z], dev(y, zz, c, x))
+        return remote(xc.at[:, window(zz)], xt.at[xt_rows, :], xts.at[i], xtr.at[c, z], dev(y, zz, 0, x))
 
     late = (3, 8, 13)
 
@@ -304,13 +306,12 @@
         for i in range(1, NZ):
             if i not in late:
                 to_column(i).start()
+        xt[xt_rows, :] = xc[:, window(z)]
 
     @pl.when(c == 1)
     def _():
-        for i in range(1, NZ):
+        for i in range(NZ):
             to_column(i).start()
-
-    xt[xt_rows, :] = xc[:, window(z)]
 
     def to_sibling():
         return remote(lsum, lsum, dls, dlr, dev(0, z, 1, x))
@@ -327,11 +328,18 @@
             outsem_s.at[i], outsem_r.at[head], dev(yy, z, cc, x),
         )
 
-    def to_all(i):
-        p = (me + i) % 8
-        return remote(
-            gl.at[p // 2], lgx.at[mine], gs.at[i], gr.at[mine], dev(p // 2, z, p % 2, (x + i // 8) % NX)
-        )
+    def to_rows(t, k):
+        return remote(gl.at[t], lgx.at[mine], gs.at[t, k], gr.at[mine], dev(t, z, 0, (x + k) % NX))
+
+    def each_rows(t, act):
+        for k in range(NX):
+            if k == 0:
+
+                @pl.when((y != t) | (c != 0))
+                def _():
+                    act(to_rows(t, k))
+            else:
+                act(to_rows(t, k))
 
     @pl.when(is_owner)
     def _():
@@ -347,20 +355,6 @@
                 for zz in range(NZ):
                     ref = gat.at[0:2, yy, zz]
                     remote(ref, ref, qfs.at[0, 0], fr.at[0, yy, zz], dev(yy, z, 1, x)).wait_recv()
-
-        for t in range(16):
-            cols = slice(t * 128, (t + 1) * 128)
-            row16 = iota((16, 128), 0)
-            lane16 = iota((16, 128), 1)
-            value = jnp.where(row16 == 0, t * 8 + lane16 // 16, jnp.where(row16 == 1, lane16 % 16, 0))
-            ownx[:, cols] = value.astype(F32).astype(BF16)
-        own = dot(sel[...], ownx[...], 1, 1)
-        own_j = own[:, 0:1] * 16.0 + own[:, 1:2]
-        own_j_row = jnp.transpose(jnp.broadcast_to(own_j, (128, 128)))[0:1]
-
-        selw = sel[...]
-        q_own = dot(selw, all_rows(Q), 1, 0).astype(BF16)
-        k_own = dot(selw, all_rows(K), 1, 0).astype(BF16)
 
         for t in range(4):
             cols = slice(t * 512, (t + 1) * 512)
@@ -375,21 +369,11 @@
             total = jnp.zeros((1, 512), F32)
             for u in range(t + 1):
                 keys = slice(u * 512, (u + 1) * 512)
-                weight = jnp.exp((st[keys, :] - most) * SCALE)
+                weight = jnp.exp2((st[keys, :] - most) * SCALE2)
                 total = total + jnp.sum(weight, axis=0, keepdims=True)
                 wt[keys, cols] = weight.astype(BF16)
-            rows[0:1, cols] = most * SCALE + jnp.log(total)
+            rows[0:1, cols] = most * SCALE2 + jnp.log2(total)
             rows[3:4, cols] = 1.0 / total
-
-        score = dot(all_rows(K), q_own, 1, 1)
-        score = jnp.where(iota((ROWS, 128), 0).astype(F32) <= own_j_row, score, -jnp.inf)
-        most = jnp.max(score, axis=0, keepdims=True)
-        weight = jnp.exp((score - most) * SCALE)
-        wo[...] = (weight * (1.0 / jnp.sum(weight, axis=0, keepdims=True))).astype(BF16)
-
-        score = dot(k_own, all_rows(Q), 1, 1) * SCALE
-        causal = iota((128, ROWS), 1).astype(F32) >= own_j
-        w2[...] = jnp.exp(jnp.where(causal, score - rows[0:1, :], -jnp.inf)).astype(BF16)
 
         @pl.when(c == 0)
         def _():
@@ -415,7 +399,6 @@
 
         for t in range(16):
             cols = slice(t * 128, (t + 1) * 128)
-            ownx[:, cols] = jnp.broadcast_to(lsum[t : t + 1, :], (16, 128)).astype(BF16)
             rows[2:3, cols] = jax.nn.sigmoid(lsum[t : t + 1, :])
 
         vt[...] = jnp.transpose(all_rows(V))
@@ -423,25 +406,50 @@
             part_rows = slice(t * 512, (t + 1) * 512)
             block = dot(pt[part_rows, :], all_rows(G), 1, 0)
             gc[part_rows, :] = block.astype(BF16)
-            gct[:, part_rows] = jnp.transpose(block)
-        for t in range(4):
+            gct[:, part_rows] = jnp.transpose(block.astype(BF16))
+        pl.semaphore_wait(xready, 3)
+        for t in (3, 2, 1, 0):
             cols = slice(t * 512, (t + 1) * 512)
             n = (t + 1) * 512
             ctx = dot(vt[:, :n], wt[:n, cols], 1, 0)
-            gate_part = jnp.sum(ctx * gct[:, cols], axis=0, keepdims=True) * rows[3:4, cols]
+            gate_part = jnp.sum(ctx * gct[:, cols].astype(F32), axis=0, keepdims=True) * rows[3:4, cols]
             gating = rows[2:3, cols]
             rows[1:2, cols] = gating * gate_part
             logit_grad = gate_part * gating * (1.0 - gating)
             for u in range(4):
                 gl[t, u : u + 1, :] = logit_grad[:, u * 128 : (u + 1) * 128]
             gl[t, 4:8, :] = jnp.zeros((4, 128), F32)
-        pl.semaphore_wait(xready, 3)
-        for i in range(1, 32):
-            to_all(i).start()
-        lgx[mine] = gl[y]
-
+            each_rows(t, lambda copy: copy.start())
+
+        @pl.when(c == 0)
+        def _():
+            lgx[mine] = gl[y]
+
+        for t in range(16):
+            cols = slice(t * 128, (t + 1) * 128)
+            row16 = iota((16, 128), 0)
+            lane16 = iota((16, 128), 1)
+            value = jnp.where(row16 == 0, t * 8 + lane16 // 16, jnp.where(row16 == 1, lane16 % 16, 0))
+            ownx[:, cols] = jnp.where(row16 == 2, lsum[t : t + 1, :], value.astype(F32)).astype(BF16)
         own = dot(sel[...], ownx[...], 1, 1)
-        own_gate = jax.nn.sigmoid(jnp.transpose(jnp.broadcast_to(own[:, 0:1], (128, 128)))[0:1])
+        own_j = own[:, 0:1] * 16.0 + own[:, 1:2]
+        own_j_row = jnp.transpose(jnp.broadcast_to(own_j, (128, 128)))[0:1]
+        own_gate = jax.nn.sigmoid(jnp.transpose(jnp.broadcast_to(own[:, 2:3], (128, 128)))[0:1])
+
+        selw = sel[...]
+        q_own = dot(selw, all_rows(Q), 1, 0).astype(BF16)
+        k_own = dot(selw, all_rows(K), 1, 0).astype(BF16)
+
+        score = dot(all_rows(K), q_own, 1, 1)
+        score = jnp.where(iota((ROWS, 128), 0).astype(F32) <= own_j_row, score, -jnp.inf)
+        most = jnp.max(score, axis=0, keepdims=True)
+        weight = jnp.exp2((score - most) * SCALE2)
+        wo[...] = (weight * (1.0 / jnp.sum(weight, axis=0, keepdims=True))).astype(BF16)
+
+        score = dot(k_own, all_rows(Q), 1, 1) * SCALE2
+        causal = iota((128, ROWS), 1).astype(F32) >= own_j
+        w2[...] = jnp.exp2(jnp.where(causal, score - rows[0:1, :], -jnp.inf)).astype(BF16)
+
         v_own = dot(selw, all_rows(V), 1, 0).astype(BF16)
         g_own = gat[G, :, z].reshape(128, HD)
         ctx = dot(vt[...], wo[...], 1, 0)
@@ -466,56 +474,56 @@
     def _():
         pl.semaphore_wait(xready, 3)
 
-    for i in range(1, NZ):
-        zz = (z + i) % NZ
-        got = xt.at[pl.ds(pl.multiple_of(zz * 32 + c * CAP, CAP), CAP), :]
-        remote(got, got, xts.at[0], xtr.at[zz], dev(y, zz, c, x)).wait_recv()
-    for p in range(20):
-        xx, h = p // 5, p % 5
-        yy, cc = (h, 0) if h < 4 else (0, 1)
-
-        @pl.when((p != mine) | jnp.logical_not(is_owner))
-        def _():
-            remote(lgx.at[p], lgx.at[p], gs.at[0], gr.at[p], dev(yy, z, cc, xx)).wait_recv()
-
-    logit_grad = lgx[0]
-    for p in range(1, 20):
-        logit_grad = logit_grad + lgx[p]
-    total = jnp.zeros((8, 256), F32)
-    for t in range(4):
-        line = jnp.broadcast_to(logit_grad[t : t + 1, :], (8, 128))
-        total = total + lax.dot_general(
-            line, xt[t * 128 : (t + 1) * 128, :].astype(F32), (((1,), (0,)), ((), ())),
-            precision=lax.Precision.HIGHEST, preferred_element_type=F32,
-        )
-    part[...] = total
-
     def to_part(xx, cc):
-        return remote(part, pr.at[me], prs.at[xx, cc], prr.at[me], dev(x, z, cc, xx))
-
-    def is_me(xx, cc):
-        return (y == x) & (x == xx) & (c == cc)
-
-    for xx in range(4):
+        return remote(part, pr.at[y], prs.at[xx, cc], prr.at[y], dev(x, z, cc, xx))
+
+    def each_part(act):
+        for xx in range(4):
+            for cc in range(2):
+
+                @pl.when((y != x) | (x != xx) | (cc != 0))
+                def _():
+                    act(to_part(xx, cc))
+
+    @pl.when(c == 0)
+    def _():
         for cc in range(2):
-
-            @pl.when(jnp.logical_not(is_me(xx, cc)))
+            for i in range(1 - cc, NZ):
+                zz = (z + i) % NZ
+                got = xt.at[pl.ds(pl.multiple_of(zz * 32 + cc * CAP, CAP), CAP), :]
+                remote(got, got, xts.at[0], xtr.at[cc, zz], dev(y, zz, cc, x)).wait_recv()
+        for p in range(20):
+            xx, h = p // 5, p % 5
+            yy, cc = (h, 0) if h < 4 else (0, 1)
+
+            @pl.when(p != mine)
             def _():
-                to_part(xx, cc).start()
-
-    @pl.when(y == x)
-    def _():
-        pr[me] = part[...]
-
-    for p in range(8):
-
-        @pl.when((p != me) | (y != x))
-        def _():
-            remote(pr.at[p], pr.at[p], prs.at[0, 0], prr.at[p], dev(p // 2, z, p % 2, y)).wait_recv()
-
-    total = pr[0]
-    for p in range(1, 8):
-        total = total + pr[p]
+                remote(lgx.at[p], lgx.at[p], gs.at[0, 0], gr.at[p], dev(yy, z, cc, xx)).wait_recv()
+
+        logit_grad = lgx[0]
+        for p in range(1, 20):
+            logit_grad = logit_grad + lgx[p]
+        total = jnp.zeros((8, 256), F32)
+        for t in range(4):
+            line = jnp.broadcast_to(logit_grad[t : t + 1, :], (8, 128))
+            total = total + lax.dot_general(
+                line, xt[t * 128 : (t + 1) * 128, :].astype(F32), (((1,), (0,)), ((), ())),
+                precision=lax.Precision.HIGHEST, preferred_element_type=F32,
+            )
+        part[...] = total
+        each_part(lambda copy: copy.start())
+
+        @pl.when(y == x)
+        def _():
+            pr[y] = part[...]
+
+    for p in range(4):
+
+        @pl.when((p != y) | (y != x) | (c != 0))
+        def _():
+            remote(pr.at[p], pr.at[p], prs.at[0, 0], prr.at[p], dev(p, z, 0, y)).wait_recv()
+
+    total = pr[0] + pr[1] + pr[2] + pr[3]
     offset = (z * 80) % 128 + c * 40
     router_ref[...] = pltpu.roll(total, (256 - offset) % 256, 1)[:, :128]
 
@@ -573,19 +581,20 @@
     for i in range(1, NZ):
         to_column(i).wait_send()
 
+    @pl.when(c == 1)
+    def _():
+        to_column(0).wait_send()
+
     @pl.when(is_owner)
     def _():
         for i in range(1, 8):
             to_slot_owner(i).wait_send()
-        for i in range(1, 32):
-            to_all(i).wait_send()
-
-    for xx in range(4):
-        for cc in range(2):
-
-            @pl.when(jnp.logical_not(is_me(xx, cc)))
-            def _():
-                to_part(xx, cc).wait_send()
+        for t in range(4):
+            each_rows(t, lambda copy: copy.wait_send())
+
+    @pl.when(c == 0)
+    def _():
+        each_part(lambda copy: copy.wait_send())
 
 
 def body(stream, queries, keys, values, router_weight, chosen, owner, grad_out):
@@ -617,7 +626,7 @@
         pltpu.VMEM((ROWS, 128), BF16),
         pltpu.VMEM((128, ROWS), BF16),
         pltpu.VMEM((HD, ROWS), BF16),
-        pltpu.VMEM((HD, ROWS), F32),
+        pltpu.VMEM((HD, ROWS), BF16),
         pltpu.VMEM((ROWS, HD), BF16),
         pltpu.VMEM((8, ROWS), F32),
         pltpu.VMEM((4, 128, HD), BF16),
@@ -625,10 +634,10 @@
         pltpu.VMEM((NY, 8, 128), F32),
         pltpu.VMEM((20, 8, 128), F32),
         pltpu.VMEM((8, 256), F32),
-        pltpu.VMEM((8, 8, 256), F32),
+        pltpu.VMEM((4, 8, 256), F32),
         dma((7,)), dma((4, 2)), dma((8,)), dma, dma, dma((4,)), dma((8,)),
         dma((2, 4, 9)), dma((2, 4, 9)), dma((2, 16)), dma((2, 16)), dma((2, 16)), dma((2, 4, 16)), dma, dma,
-        dma((16,)), dma((16,)), dma((8,)), dma((5,)), dma((32,)), dma((20,)), dma((4, 2)), dma((8,)),
+        dma((16,)), dma((2, 16)), dma((8,)), dma((5,)), dma((4, 4)), dma((20,)), dma((4, 2)), dma((4,)),
         pltpu.SemaphoreType.REGULAR,
     ]
     out, router = pl.pallas_call(

time: 70 us -> 67.9 us (0.970)
  Pallas kernels: 69.2 us -> 67 us
    pallas_call x1, Pallas kernels: 67.6 us -> 65.5 us  [body(): pl.pallas_call(kernel, out_shape=(jax.ShapeDtypeStruct((4, CAP, 5 * HD),...]
where the time goes in v4:
time: 67.9 us; the launch traced here: 67.7 us
  Pallas kernels  67 us (99%)
    pallas_call x1, Pallas kernels, body(): pl.pallas_call(kernel, out_shape=(jax.ShapeDtypeStruct((4, CAP, 5 * HD),...  65.5 us
    pallas_call x1, Pallas kernels, body(): pl.pallas_call(split, out_shape=(wide, wide, wide, wide, jax.ShapeDtypeSt...  1.52 us

profile of v4, /device:TPU:1, one launch (start us, length us, event | category | flops | bytes accessed | tf_op | source)
XLA Modules:
  0.0 67.7 jit_solution(16324331193291415116)
XLA Ops:
  0.6 65.5 %routed_attention.1 = (bf16[4,16,640]{2,1,0:T(8,128)(2,1)}, f32[8,128]{1,0:T(8,128)}) custom-call(s32[2048]{0:T(1024)} %chosen_ref.1, s32[16,128]{1,0:T(8,128)} %bitcast.1, bf16[5120]{0:T(1024)(128)(2,1)} %weight_in.1, bf16[128,640]{1,0:T(8,128)(2,1)} %q_in.1, bf16[128,640]{1,0:T(8,128)(2,1)} %k_in.1, bf16[128,640]{1,0:T(8,128)(2,1)} %v_in.1, ...), custom_call_target="tpu_custom_call" | custom-call | tf_op jit(solution)/shard_map/routed_attention/pallas_call | solution.py:643
  66.1 1.5 %split_outputs.1 = (bf16[16,640]{1,0:T(8,128)(2,1)}, bf16[16,640]{1,0:T(8,128)(2,1)}, bf16[16,640]{1,0:T(8,128)(2,1)}, bf16[16,640]{1,0:T(8,128)(2,1)}, f32[40]{0:T(128)}) custom-call(bf16[4,16,640]{2,1,0:T(8,128)(2,1)} %get-tuple-element.7.out_ref, f32[8,128]{1,0:T(8,128)} %get-tuple-element.8.router_in), custom_call_target="tpu_custom_call" | custom-call | tf_op jit(solution)/shard_map/split_outputs/pallas_call | solution.py:667

commit v5 on v4

--- a/solution.py
+++ b/solution.py
@@ -356,22 +356,26 @@
                     ref = gat.at[0:2, yy, zz]
                     remote(ref, ref, qfs.at[0, 0], fr.at[0, yy, zz], dev(yy, z, 1, x)).wait_recv()
 
-        for t in range(4):
-            cols = slice(t * 512, (t + 1) * 512)
-            q_block = gat[Q, t].reshape(512, HD)
-            most = jnp.full((1, 512), -jnp.inf, F32)
+        for t in range(8):
+            cols = slice(t * 256, (t + 1) * 256)
+            n = t * 256
+            half = slice(t % 2 * 8, t % 2 * 8 + 8)
+            q_block = gat[Q, t // 2, half].reshape(256, HD)
+            if t:
+                st[:n, :] = dot(gat[K].reshape(ROWS, HD)[:n], q_block, 1, 1)
+            score = dot(gat[K, t // 2, half].reshape(256, HD), q_block, 1, 1)
+            st[n : n + 256, :] = jnp.where(iota((256, 256), 0) <= iota((256, 256), 1), score, -jnp.inf)
+            most = jnp.full((1, 256), -jnp.inf, F32)
             for u in range(t + 1):
-                score = dot(gat[K, u].reshape(512, HD), q_block, 1, 1)
-                if u == t:
-                    score = jnp.where(iota((512, 512), 0) <= iota((512, 512), 1), score, -jnp.inf)
-                st[u * 512 : (u + 1) * 512, :] = score
-                most = jnp.maximum(most, jnp.max(score, axis=0, keepdims=True))
-            total = jnp.zeros((1, 512), F32)
+                most = jnp.maximum(most, jnp.max(st[u * 256 : (u + 1) * 256, :], axis=0, keepdims=True))
+            total = jnp.zeros((1, 256), F32)
             for u in range(t + 1):
-                keys = slice(u * 512, (u + 1) * 512)
+                keys = slice(u * 256, (u + 1) * 256)
                 weight = jnp.exp2((st[keys, :] - most) * SCALE2)
                 total = total + jnp.sum(weight, axis=0, keepdims=True)
                 wt[keys, cols] = weight.astype(BF16)
+            if t % 2 == 0:
+                wt[n + 256 : n + 512, cols] = jnp.zeros((256, 256), BF16)
             rows[0:1, cols] = most * SCALE2 + jnp.log2(total)
             rows[3:4, cols] = 1.0 / total
 
@@ -505,11 +509,14 @@
             logit_grad = logit_grad + lgx[p]
         total = jnp.zeros((8, 256), F32)
         for t in range(4):
-            line = jnp.broadcast_to(logit_grad[t : t + 1, :], (8, 128))
-            total = total + lax.dot_general(
-                line, xt[t * 128 : (t + 1) * 128, :].astype(F32), (((1,), (0,)), ((), ())),
-                precision=lax.Precision.HIGHEST, preferred_element_type=F32,
-            )
+            line = logit_grad[t : t + 1, :]
+            high = line.astype(BF16).astype(F32)
+            middle = (line - high).astype(BF16).astype(F32)
+            row16 = iota((16, 128), 0)
+            terms = jnp.where(row16 == 0, high, jnp.where(row16 == 1, middle, line - high - middle))
+            terms = jnp.where(row16 < 3, terms, 0.0).astype(BF16)
+            sums = jnp.sum(dot(terms, xt[t * 128 : (t + 1) * 128, :], 1, 0), axis=0, keepdims=True)
+            total = total + jnp.broadcast_to(sums, (8, 256))
         part[...] = total
         each_part(lambda copy: copy.start())
 
@@ -621,7 +628,7 @@
         pltpu.VMEM((ROWS, ROWS), BF16),
         pltpu.VMEM((128, ROWS), BF16),
         pltpu.VMEM((16, ROWS), BF16),
-        pltpu.VMEM((ROWS, 512), F32),
+        pltpu.VMEM((ROWS, 256), F32),
         pltpu.VMEM((ROWS, ROWS), BF16),
         pltpu.VMEM((ROWS, 128), BF16),
         pltpu.VMEM((128, ROWS), BF16),

time: 67.9 us -> 67.6 us (level)
  no operation moved by 1% of the time
where the time goes in v5:
time: 67.6 us; the launch traced here: 67.4 us
  Pallas kernels  66.8 us (99%)
    pallas_call x1, Pallas kernels, body(): pl.pallas_call(kernel, out_shape=(jax.ShapeDtypeStruct((4, CAP, 5 * HD),...  65.2 us
    pallas_call x1, Pallas kernels, body(): pl.pallas_call(split, out_shape=(wide, wide, wide, wide, jax.ShapeDtypeSt...  1.52 us

profile of v5, /device:TPU:1, one launch (start us, length us, event | category | flops | bytes accessed | tf_op | source)
XLA Modules:
  0.0 67.4 jit_solution(13265773577642401803)
XLA Ops:
  0.6 65.2 %routed_attention.1 = (bf16[4,16,640]{2,1,0:T(8,128)(2,1)}, f32[8,128]{1,0:T(8,128)}) custom-call(s32[2048]{0:T(1024)} %chosen_ref.1, s32[16,128]{1,0:T(8,128)} %bitcast.1, bf16[5120]{0:T(1024)(128)(2,1)} %weight_in.1, bf16[128,640]{1,0:T(8,128)(2,1)} %q_in.1, bf16[128,640]{1,0:T(8,128)(2,1)} %k_in.1, bf16[128,640]{1,0:T(8,128)(2,1)} %v_in.1, ...), custom_call_target="tpu_custom_call" | custom-call | tf_op jit(solution)/shard_map/routed_attention/pallas_call | solution.py:650
  65.9 1.5 %split_outputs.1 = (bf16[16,640]{1,0:T(8,128)(2,1)}, bf16[16,640]{1,0:T(8,128)(2,1)}, bf16[16,640]{1,0:T(8,128)(2,1)}, bf16[16,640]{1,0:T(8,128)(2,1)}, f32[40]{0:T(128)}) custom-call(bf16[4,16,640]{2,1,0:T(8,128)(2,1)} %get-tuple-element.7.out_ref, f32[8,128]{1,0:T(8,128)} %get-tuple-element.8.router_in), custom_call_target="tpu_custom_call" | custom-call | tf_op jit(solution)/shard_map/split_outputs/pallas_call | solution.py:674
